TPU v7x, 512 devices: a whole 4x8x8 slice. The times are simulated.
512 devices in a mesh: expert: 64 (over z, y), dp: 8 (over x, core).
Axes of the slice: x: 4, y: 8, z: 8, core: 2. Of those that a mesh axis runs over, the one named last changes fastest.
Arguments:
- tokens: bfloat16 [1024, 4096], P('expert', 'dp'), may hold values from -6 to 6
- expert_ids: int32 [1024, 8], P('expert'), may hold values from 0 to 63, as said below
- route_weight: float32 [1024, 8], P('expert'), may hold values from 0.05 to 0.5
- placement: int32 [4], replicated, may hold values from 0 to 63, as said below
- gate_up_base: bfloat16 [64, 4096, 2048], P('expert', 'dp'), may hold values from -0.09375 to 0.09375
- down_base: bfloat16 [64, 1024, 4096], P('expert', None, 'dp'), may hold values from -0.1875 to 0.1875
- gate_up_a: bfloat16 [64, 4096, 128], P('expert', 'dp'), may hold values from -0.09375 to 0.09375
- gate_up_b: bfloat16 [64, 128, 1024], P('expert'), may hold values from -0.75 to 0.75
- down_a: bfloat16 [64, 1024, 64], P('expert'), may hold values from -0.1875 to 0.1875
- down_b: bfloat16 [64, 64, 4096], P('expert', None, 'dp'), may hold values from -0.75 to 0.75
- grad_mixed: bfloat16 [1024, 4096], P('expert', 'dp'), may hold values from -6 to 6
Outputs:
- mixed: bfloat16 [1024, 4096], P('expert', 'dp')
- grad_tokens: bfloat16 [1024, 4096], P('expert', 'dp')
- grad_gate_up_a: float32 [64, 4096, 128], P('expert', 'dp')
- grad_gate_up_b: float32 [64, 128, 1024], P('expert')
- grad_down_a: float32 [64, 1024, 64], P('expert')
- grad_down_b: float32 [64, 64, 4096], P('expert', None, 'dp')
- column_rows: int32 [64], P('expert')
- column_blocks: int32 [64], P('expert')
Inputs may be any that keep to these rules, and one draw needn't show every extreme that they name: `expert_ids`: every device's 16 tokens name expert placement[0] exactly 8 times and each other expert at most 2 times; the 8 experts of one token are distinct. placement[0] is the hot expert; the other 3 entries are distinct indices of the expert axis, none equal to placement[0]; index 63 is always among the entries.
All inputs are finite; a program needn't handle non-finite values.
Results may differ from a plain program's by a relative error of at most 0.03.
Values may be sent and summed in bfloat16 or wider, within the bound.
A program may use at most 64 MiB of HBM per device.

v0:
```python
import jax
import jax.numpy as jnp
from jax import lax
from jax.sharding import PartitionSpec as P

adapter_scale = 0.25


def trailing_product(left, right):
    return lax.dot_general(
        left, right, (((1,), (1,)), ((), ())), preferred_element_type=jnp.float32
    )


def leading_product(left, right):
    return lax.dot_general(
        left, right, (((0,), (0,)), ((), ())), preferred_element_type=jnp.float32
    )


def dispatch(buffer):
    return lax.all_to_all(buffer, "expert", split_axis=0, concat_axis=0, tiled=True)


def collect(buffer):
    return lax.all_to_all(buffer, "expert", split_axis=0, concat_axis=0, tiled=True)


def place_rows(slot_rows, slot_target, total_rows):
    return (
        jnp.zeros((total_rows, slot_rows.shape[1]), slot_rows.dtype).at[slot_target].set(slot_rows)
    )


def expert_forward(row_features, weights):
    (
        frozen_gate_up_weight,
        frozen_down_weight,
        lowrank_input,
        lowrank_output,
        down_adapter_input,
        down_adapter_output,
    ) = weights
    hidden_unit_width = frozen_down_weight.shape[0]
    rank_width = down_adapter_input.shape[1]
    partial_value = jnp.dot(row_features, frozen_gate_up_weight, preferred_element_type=jnp.float32)
    low_part = jnp.dot(row_features, lowrank_input, preferred_element_type=jnp.float32)
    reduced_sum, low_sum = (
        lax.psum(partial_value.astype(jnp.bfloat16), "dp").astype(jnp.float32),
        lax.psum(low_part.astype(jnp.bfloat16), "dp").astype(jnp.float32),
    )
    lowrank_value = low_sum.astype(jnp.bfloat16)
    gate_activation = reduced_sum[:, :hidden_unit_width] + adapter_scale * jnp.dot(
        lowrank_value[:, :rank_width],
        lowrank_output[:rank_width],
        preferred_element_type=jnp.float32,
    )
    up_projection_value = reduced_sum[:, hidden_unit_width:] + adapter_scale * jnp.dot(
        lowrank_value[:, rank_width:],
        lowrank_output[rank_width:],
        preferred_element_type=jnp.float32,
    )
    sigmoid_gate = jax.nn.sigmoid(gate_activation)
    hidden_activation = (gate_activation * sigmoid_gate * up_projection_value).astype(jnp.bfloat16)
    hidden_lowrank = jnp.dot(
        hidden_activation, down_adapter_input, preferred_element_type=jnp.float32
    ).astype(jnp.bfloat16)
    layer_output = (
        jnp.dot(hidden_activation, frozen_down_weight, preferred_element_type=jnp.float32)
        + adapter_scale
        * jnp.dot(hidden_lowrank, down_adapter_output, preferred_element_type=jnp.float32)
    ).astype(jnp.bfloat16)
    return (
        layer_output,
        (
            row_features,
            lowrank_value,
            gate_activation,
            up_projection_value,
            sigmoid_gate,
            hidden_activation,
            hidden_lowrank,
        ),
    )


def expert_backward(slot_gradient_rows, saved, weights):
    (
        frozen_gate_up_weight,
        frozen_down_weight,
        lowrank_input,
        lowrank_output,
        down_adapter_input,
        down_adapter_output,
    ) = weights
    (
        row_features,
        lowrank_value,
        gate_activation,
        up_projection_value,
        sigmoid_gate,
        hidden_activation,
        hidden_lowrank,
    ) = saved
    hidden_unit_width = frozen_down_weight.shape[0]
    rank_width = down_adapter_input.shape[1]
    back_part = trailing_product(slot_gradient_rows, frozen_down_weight)
    back_low_part = trailing_product(slot_gradient_rows, down_adapter_output)
    backward_total, back_low_sum = (
        lax.psum(back_part.astype(jnp.bfloat16), "dp").astype(jnp.float32),
        lax.psum(back_low_part.astype(jnp.bfloat16), "dp").astype(jnp.float32),
    )
    backward_lowrank = back_low_sum.astype(jnp.bfloat16)
    gradient_hidden_units = backward_total + adapter_scale * trailing_product(
        backward_lowrank, down_adapter_input
    )
    gradient_down_adapter_output = adapter_scale * leading_product(
        hidden_lowrank, slot_gradient_rows
    )
    gradient_down_adapter_input = adapter_scale * leading_product(
        hidden_activation, backward_lowrank
    )
    activated = gate_activation * sigmoid_gate
    grad_gate = (
        gradient_hidden_units
        * up_projection_value
        * sigmoid_gate
        * (1.0 + gate_activation * (1.0 - sigmoid_gate))
    )
    grad_up = gradient_hidden_units * activated
    gradient_gate_up_pair = jnp.concatenate([grad_gate, grad_up], 1).astype(jnp.bfloat16)
    gradient_lowrank_output = adapter_scale * jnp.concatenate(
        [
            leading_product(
                lowrank_value[:, :rank_width], gradient_gate_up_pair[:, :hidden_unit_width]
            ),
            leading_product(
                lowrank_value[:, rank_width:], gradient_gate_up_pair[:, hidden_unit_width:]
            ),
        ],
        0,
    )
    lowrank_backward = jnp.concatenate(
        [
            trailing_product(
                gradient_gate_up_pair[:, :hidden_unit_width], lowrank_output[:rank_width]
            ),
            trailing_product(
                gradient_gate_up_pair[:, hidden_unit_width:], lowrank_output[rank_width:]
            ),
        ],
        1,
    ).astype(jnp.bfloat16)
    gradient_lowrank_input = adapter_scale * leading_product(row_features, lowrank_backward)
    gradient_row_block = (
        trailing_product(gradient_gate_up_pair, frozen_gate_up_weight)
        + adapter_scale * trailing_product(lowrank_backward, lowrank_input)
    ).astype(jnp.bfloat16)
    return (
        gradient_row_block,
        (
            gradient_lowrank_input,
            gradient_lowrank_output,
            gradient_down_adapter_input,
            gradient_down_adapter_output,
        ),
    )


def per_device(
    tokens,
    expert_ids,
    route_weight,
    placement,
    gate_up_base,
    down_base,
    gate_up_a,
    gate_up_b,
    down_a,
    down_b,
    grad_mixed,
):
    expert_count = lax.axis_size("expert")
    own_index = lax.axis_index("expert")
    token_count, topk_count = expert_ids.shape
    feature_width = tokens.shape[1]
    slot_count = token_count * topk_count
    copy_count = placement.shape[0] - 1
    hot_limit = min(token_count, max(2, 4 * token_count * topk_count // expert_count))
    other_limit = (token_count * topk_count - hot_limit + expert_count - 2) // (expert_count - 1)
    hot_expert = placement[0]
    flat_ids = expert_ids.reshape(-1)
    columns = jnp.arange(expert_count, dtype=jnp.int32)
    own_weights = (gate_up_base[0], down_base[0], gate_up_a[0], gate_up_b[0], down_a[0], down_b[0])
    host_col = placement[own_index * (copy_count + 1) // expert_count]
    destination = jnp.where(flat_ids == hot_expert, host_col, flat_ids)
    dest_counts = jnp.sum((destination[:, None] == columns[None, :]).astype(jnp.int32), 0)
    all_counts = lax.psum(dest_counts, "expert")
    own_count = all_counts[own_index]
    column_rows = own_count[None]
    column_blocks = ((own_count + 127) // 128)[None]
    token_slots = jnp.repeat(tokens, topk_count, axis=0)
    grad_slots = (
        (route_weight[:, :, None] * grad_mixed[:, None, :].astype(jnp.float32))
        .astype(jnp.bfloat16)
        .reshape(slot_count, feature_width)
    )
    capacity = max(hot_limit, other_limit)
    onehot = (flat_ids[:, None] == columns[None, :]).astype(jnp.int32)
    slot_rank = jnp.sum((jnp.cumsum(onehot, 0) - 1) * onehot, 1)
    slot_target = flat_ids * capacity + slot_rank
    total_rows = expert_count * capacity
    arrived = dispatch(
        place_rows(token_slots, slot_target, total_rows).reshape(
            expert_count, capacity, feature_width
        )
    )
    layer_output, saved = expert_forward(arrived.reshape(total_rows, feature_width), own_weights)
    returned = collect(layer_output.reshape(expert_count, capacity, feature_width)).reshape(
        total_rows, feature_width
    )
    arrived_grad = dispatch(
        place_rows(grad_slots, slot_target, total_rows).reshape(
            expert_count, capacity, feature_width
        )
    )
    gradient_row_block, expert_grads = expert_backward(
        arrived_grad.reshape(total_rows, feature_width), saved, own_weights
    )
    returned_grad = collect(
        gradient_row_block.reshape(expert_count, capacity, feature_width)
    ).reshape(total_rows, feature_width)
    slot_out = (
        returned[slot_target].reshape(token_count, topk_count, feature_width).astype(jnp.float32)
    )
    mixed = jnp.sum(route_weight[:, :, None] * slot_out, 1).astype(jnp.bfloat16)
    slot_back = (
        returned_grad[slot_target]
        .reshape(token_count, topk_count, feature_width)
        .astype(jnp.float32)
    )
    grad_tokens = jnp.sum(slot_back, 1).astype(jnp.bfloat16)
    (
        gradient_lowrank_input,
        gradient_lowrank_output,
        gradient_down_adapter_input,
        gradient_down_adapter_output,
    ) = expert_grads
    return (
        mixed,
        grad_tokens,
        gradient_lowrank_input[None],
        gradient_lowrank_output[None],
        gradient_down_adapter_input[None],
        gradient_down_adapter_output[None],
        column_rows,
        column_blocks,
    )


def solution(mesh):
    return jax.shard_map(
        per_device,
        mesh=mesh,
        in_specs=(
            P("expert", "dp"),
            P("expert", None),
            P("expert", None),
            P(),
            P("expert", "dp", None),
            P("expert", None, "dp"),
            P("expert", "dp", None),
            P("expert", None, None),
            P("expert", None, None),
            P("expert", None, "dp"),
            P("expert", "dp"),
        ),
        out_specs=(
            P("expert", "dp"),
            P("expert", "dp"),
            P("expert", "dp", None),
            P("expert", None, None),
            P("expert", None, None),
            P("expert", None, "dp"),
            P("expert"),
            P("expert"),
        ),
        check_vma=False,
    )
```

profile of v0, /device:TPU:6, one launch (start us, length us, event | category | flops | bytes accessed | tf_op | source)
XLA Modules:
  0.0 246.4 jit_solution(6575152055103390403)
XLA Ops:
  11.1 2.0 scatter_custom_fusion.1
  13.0 16.6 %all-to-all-start.2 = ((bf16[64,8,512]{2,1,0:T(8,128)(2,1)}), bf16[64,8,512]{2,1,0:T(8,128)(2,1)S(1)}, u32[]{:S(2)}, u32[]{:S(2)}) async-start(bf16[64,8,512]{2,1,0:T(8,128)(2,1)} %bitcast.16), calls=%async_computation.2 | async-start | bytes 1048576 | tf_op jit(solution)/shard_map/all_to_all | solution.py:22
  29.6 2.1 scatter_custom_fusion
  31.7 17.6 %all-to-all-done.2 = bf16[64,8,512]{2,1,0:T(8,128)(2,1)S(1)} async-done(((bf16[64,8,512]{2,1,0:T(8,128)(2,1)}), bf16[64,8,512]{2,1,0:T(8,128)(2,1)S(1)}, u32[]{:S(2)}, u32[]{:S(2)}) %all-to-all-start.2) | async-done | bytes 524320 | tf_op jit(solution)/shard_map/all_to_all | solution.py:22
  49.4 5.0 %all-to-all-start = ((bf16[64,8,512]{2,1,0:T(8,128)(2,1)}), bf16[64,8,512]{2,1,0:T(8,128)(2,1)S(1)}, u32[]{:S(2)}, u32[]{:S(2)}) async-start(bf16[64,8,512]{2,1,0:T(8,128)(2,1)} %bitcast.103), calls=%async_computation | async-start | bytes 1048576 | tf_op jit(solution)/shard_map/all_to_all | solution.py:22
  55.3 3.0 %convolution_convert_fusion.1 = bf16[512,1024]{1,0:T(8,128)(2,1)} fusion(bf16[1,1024,512]{2,1,0:T(8,128)(2,1)} %param.16, bf16[64,8,512]{2,1,0:T(8,128)(2,1)S(1)} %all-to-all-done.2), kind=kOutput, calls=%fused_computation.19 | convolution fusion | flops 537395200 | bytes 2621440 | tf_op jit(solution)/shard_map/dot_general | solution.py:10
  58.3 14.9 %all-to-all-done = bf16[64,8,512]{2,1,0:T(8,128)(2,1)S(1)} async-done(((bf16[64,8,512]{2,1,0:T(8,128)(2,1)}), bf16[64,8,512]{2,1,0:T(8,128)(2,1)S(1)}, u32[]{:S(2)}, u32[]{:S(2)}) %all-to-all-start) | async-done | bytes 524320 | tf_op jit(solution)/shard_map/all_to_all | solution.py:22
  73.2 2.6 %convolution_convert_fusion = bf16[512,2048]{1,0:T(8,128)(2,1)} fusion(bf16[1,512,2048]{2,1,0:T(8,128)(2,1)S(1)} %copy-done, bf16[64,8,512]{2,1,0:T(8,128)(2,1)S(1)} %all-to-all-done), kind=kOutput, calls=%fused_computation.4 | convolution fusion | flops 1074790400 | bytes 4718592 | tf_op jit(solution)/shard_map/dot_general | solution.py:46
  77.3 70.8 %all-reduce.3.cloned.1.call-done = (bf16[512,2048]{1,0:T(8,128)(2,1)}, bf16[512,128]{1,0:T(8,128)(2,1)}, bf16[512,1024]{1,0:T(8,128)(2,1)}, bf16[512,64]{0,1:T(8,128)(2,1)}) async-done(((bf16[512,2048]{1,0:T(8,128)(2,1)}, bf16[512,128]{1,0:T(8,128)(2,1)}, bf16[512,1024]{1,0:T(8,128)(2,1)}, bf16[512,64]{0,1:T(8,128)(2,1)}), (bf16[512,2048]{1,0:T(8,128)(2,1)}, bf16[512,128]{1,0:T(8,128)(2,1)}, ...) | async-done | bytes 3342352 | tf_op jit(solution)/shard_map/psum | solution.py:49
  148.2 2.2 convert_element_type.63
  152.0 2.3 multiply_convert_fusion.1
  155.3 1.3 fusion
  157.7 13.5 %all-to-all-start.3 = ((bf16[64,8,512]{2,1,0:T(8,128)(2,1)}), bf16[64,8,512]{2,1,0:T(8,128)(2,1)}, u32[]{:S(2)}, u32[]{:S(2)}) async-start(bf16[64,8,512]{2,1,0:T(8,128)(2,1)} %fusion.12), calls=%async_computation.3 | async-start | bytes 1048576 | tf_op jit(solution)/shard_map/all_to_all | solution.py:26
  171.3 1.3 compare_select_fusion
  172.7 31.7 %psum.39 = s32[64]{0:T(128)S(1)} all-reduce(s32[64]{0:T(128)S(1)} %convert_reduce_fusion), channel_id=1, replica_groups=mesh['expert'=64,'dp'=8] {'expert'}, use_global_device_ids=true, to_apply=%region_11.12 | all-reduce | flops 64 | bytes 512 | tf_op jit(solution)/shard_map/psum | solution.py:198
  205.7 1.7 convolution_convert_fusion.5
  207.4 2.3 fusion.17
  209.7 1.1 fusion.11
  210.8 8.3 %all-to-all-start.1 = ((bf16[64,8,512]{2,1,0:T(8,128)(2,1)}), bf16[64,8,512]{2,1,0:T(8,128)(2,1)}, u32[]{:S(2)}, u32[]{:S(2)}) async-start(bf16[64,8,512]{2,1,0:T(8,128)(2,1)} %fusion.11), calls=%async_computation.1 | async-start | bytes 1048576 | tf_op jit(solution)/shard_map/all_to_all | solution.py:26
  219.1 1.5 convolution_bitcast_fusion.1
  220.7 1.7 convolution_bitcast_fusion
  226.1 2.0 gather_fusion.1
  228.8 6.9 %all-to-all-done.1 = bf16[64,8,512]{2,1,0:T(8,128)(2,1)} async-done(((bf16[64,8,512]{2,1,0:T(8,128)(2,1)}), bf16[64,8,512]{2,1,0:T(8,128)(2,1)}, u32[]{:S(2)}, u32[]{:S(2)}) %all-to-all-start.1) | async-done | bytes 524320 | tf_op jit(solution)/shard_map/all_to_all | solution.py:26
  235.7 2.0 gather_fusion
  (60 shorter events, 16.0 us)
Async XLA Ops:
  7.2 66.0 %copy-start = (bf16[1,512,2048]{2,1,0:T(8,128)(2,1)S(1)}, bf16[1,512,2048]{2,1,0:T(8,128)(2,1)}, u32[]{:S(2)}) copy-start(bf16[1,512,2048]{2,1,0:T(8,128)(2,1)} %param.15) | copy-start | bytes 6291460
  7.2 47.2 %copy-start.9 = (bf16[1,64,512]{2,1,0:T(8,128)(2,1)S(1)}, bf16[1,64,512]{2,1,0:T(8,128)(2,1)}, u32[]{:S(2)}) copy-start(bf16[1,64,512]{2,1,0:T(8,128)(2,1)} %param.20) | copy-start | bytes 196612
  13.0 36.3 %all-to-all-start.2 = ((bf16[64,8,512]{2,1,0:T(8,128)(2,1)}), bf16[64,8,512]{2,1,0:T(8,128)(2,1)S(1)}, u32[]{:S(2)}, u32[]{:S(2)}) async-start(bf16[64,8,512]{2,1,0:T(8,128)(2,1)} %bitcast.16), calls=%async_computation.2 | async-start | bytes 1048576 | tf_op jit(solution)/shard_map/all_to_all | solution.py:22
  49.4 23.8 %all-to-all-start = ((bf16[64,8,512]{2,1,0:T(8,128)(2,1)}), bf16[64,8,512]{2,1,0:T(8,128)(2,1)S(1)}, u32[]{:S(2)}, u32[]{:S(2)}) async-start(bf16[64,8,512]{2,1,0:T(8,128)(2,1)} %bitcast.103), calls=%async_computation | async-start | bytes 1048576 | tf_op jit(solution)/shard_map/all_to_all | solution.py:22
  54.4 93.8 %all-reduce.3.cloned.1.call-start = ((), (), s32[]{:S(2)}) async-start(), calls=%async_computation.4 | async-start | bytes 6684672 | tf_op jit(solution)/shard_map/psum | solution.py:49
  58.3 17.4 %copy-start.7 = (bf16[1,512,128]{2,1,0:T(8,128)(2,1)S(1)}, bf16[1,512,128]{2,1,0:T(8,128)(2,1)}, u32[]{:S(2)}) copy-start(bf16[1,512,128]{2,1,0:T(8,128)(2,1)} %param.17) | copy-start | bytes 393220
  75.8 1.0 copy-start.13
  148.2 2.2 copy-start.4
  148.2 2.2 copy-start.6
  150.4 1.2 copy-start.5
  150.4 1.2 copy-start.8
  150.4 1.2 copy-start.11
  154.4 2.2 copy-start.2
  154.4 2.2 copy-start.3
  157.7 53.1 %all-to-all-start.3 = ((bf16[64,8,512]{2,1,0:T(8,128)(2,1)}), bf16[64,8,512]{2,1,0:T(8,128)(2,1)}, u32[]{:S(2)}, u32[]{:S(2)}) async-start(bf16[64,8,512]{2,1,0:T(8,128)(2,1)} %fusion.12), calls=%async_computation.3 | async-start | bytes 1048576 | tf_op jit(solution)/shard_map/all_to_all | solution.py:26
  205.7 4.0 %copy-start.10 = (bf16[1,64,512]{2,1,0:T(8,128)(2,1)S(1)}, bf16[1,64,512]{2,1,0:T(8,128)(2,1)}, u32[]{:S(2)}) copy-start(bf16[1,64,512]{2,1,0:T(8,128)(2,1)} %param.20) | copy-start | bytes 196612
  210.8 24.9 %all-to-all-start.1 = ((bf16[64,8,512]{2,1,0:T(8,128)(2,1)}), bf16[64,8,512]{2,1,0:T(8,128)(2,1)}, u32[]{:S(2)}, u32[]{:S(2)}) async-start(bf16[64,8,512]{2,1,0:T(8,128)(2,1)} %fusion.11), calls=%async_computation.1 | async-start | bytes 1048576 | tf_op jit(solution)/shard_map/all_to_all | solution.py:26
  220.7 4.5 %copy-start.1 = (bf16[512,1024]{1,0:T(8,128)(2,1)S(1)}, bf16[512,1024]{1,0:T(8,128)(2,1)}, u32[]{:S(2)}) copy-start(bf16[512,1024]{1,0:T(8,128)(2,1)} %get-tuple-element.14) | copy-start | bytes 3145732
  220.7 4.5 %copy-start.12 = (bf16[512,64]{0,1:T(8,128)(2,1)S(1)}, bf16[512,64]{0,1:T(8,128)(2,1)}, u32[]{:S(2)}) copy-start(bf16[512,64]{0,1:T(8,128)(2,1)} %get-tuple-element.11) | copy-start | bytes 196612
Sparse Core Ops, SparseCore 0:
  76.9 71.2 all-reduce.2
where the time goes:
time: 247 us; the launch traced here: 246 us
  waiting for transfers between devices  110 us (45%)
  starting transfers between devices  43.5 us (18%)
  blocking collectives  31.7 us (13%)
  matrix products  25.2 us (10%)
  between operations  16.1 us (7%)
  local copies, waits for them, and re-layouts  10 us (4%)
  other arithmetic  9.64 us (4%)
    psum x1, waiting for transfers between devices, expert_forward(): lax.psum(partial_value.astype(jnp.bfloat16), 'dp').astype(jnp.float32)  70.8 us
    all_to_all x2, waiting for transfers between devices, dispatch(): lax.all_to_all(buffer, 'expert', split_axis=0, concat_axis=0, tiled=True)  32.5 us
    psum x1, blocking collectives, per_device(): all_counts = lax.psum(dest_counts, 'expert')  31.7 us
    all_to_all x2, starting transfers between devices, collect(): lax.all_to_all(buffer, 'expert', split_axis=0, concat_axis=0, tiled=True)  21.8 us
    all_to_all x2, starting transfers between devices, dispatch(): lax.all_to_all(buffer, 'expert', split_axis=0, concat_axis=0, tiled=True)  21.6 us
    dot_general x7, matrix products, trailing_product(): lax.dot_general(left, right, (((1,), (1,)), ((), ())), preferred_element_...  7.64 us
    all_to_all x2, waiting for transfers between devices, collect(): lax.all_to_all(buffer, 'expert', split_axis=0, concat_axis=0, tiled=True)  6.9 us
    dot_general x5, matrix products, leading_product(): lax.dot_general(left, right, (((0,), (0,)), ((), ())), preferred_element_...  6.15 us
  transfers between devices with their start and end apart: 5, of which 4 were waited for; matrix products, arithmetic and copies ran while one was open for 9% of the time, Pallas kernels for 0%

commit v1 on v0

v1 whole, which is shorter than its diff:
```python
import jax
import jax.numpy as jnp
from jax import lax
from jax.experimental import pallas as pl
from jax.experimental.pallas import tpu as pltpu
from jax.sharding import PartitionSpec as P

SCALE = 0.25
BF = jnp.bfloat16
F32 = jnp.float32
NY, NZ, NX = 8, 8, 4
COLS = NY * NZ
TOK = 16
DF = 512
HID = 1024
PARTS = 5
ROWS = 128
BLK = 16
LANE = 128
C_LOW, C_BACK, C_BL, WP = 2048, 2176, 3200, 3328
HALF = 1664
A_GB, A_LB, A_LOW, A_HB, WA = 1024, 3072, 3200, 3328, 3456
AHALF = 1792
HW = 640
TICKS = PARTS + 6


def dot(a, b):
    return jnp.dot(a, b, preferred_element_type=F32)


def dot_t(a, b):
    return lax.dot_general(a, b, (((1,), (1,)), ((), ())), preferred_element_type=F32)


def t_dot(a, b):
    return lax.dot_general(a, b, (((0,), (0,)), ((), ())), preferred_element_type=F32)


def kernel(
    tok, ids, rw, grad, plc, gu_h, dn_h, ga_h, gb_h, da_h, db_h,
    mixed_o, gtok_o, gga_o, ggb_o, gda_o, gdb_o, rows_o, blocks_o,
    gu, dn, ga, gb, da, db, wsem,
    route, hroute, stage, nsend, nrecv, nback, nret, hg, xs, gs, pt, pr, ss, ra, rb, ag,
    hret, hgot, ysend, ygot,
    s_n, r_n, s_b, r_b, s_y, r_y, s_zp, r_zp, s_zm, r_zm, s_h, r_h, s_w, r_w,
    s_pair, r_pair, s_rs, r_2a, r_2b, s_ag, r_agx, r_fwd, s_core, r_core,
):
    e = lax.axis_index("expert")
    d = lax.axis_index("dp")
    z, y = e // NY, e % NY
    x, c = d // 2, d % 2

    def push(src, dst, ssem, rsem, dev):
        pltpu.make_async_remote_copy(
            src_ref=src, dst_ref=dst, send_sem=ssem, recv_sem=rsem, device_id=dev,
            device_id_type=pl.DeviceIdType.MESH,
        ).start()

    def wait(ref, sem):
        pltpu.make_async_copy(ref, ref, sem).wait()

    loads = [
        pltpu.make_async_copy(src, dst, wsem.at[i])
        for i, (src, dst) in enumerate(
            ((gu_h, gu), (dn_h, dn), (ga_h, ga), (gb_h, gb), (da_h, da), (db_h, db.at[0:64]))
        )
    ]
    for load in loads:
        load.start()

    xp = ((x + 1) % NX) * 2 + c
    xm = ((x + NX - 1) % NX) * 2 + c
    mate = x * 2 + (1 - c)

    barrier = pltpu.get_barrier_semaphore()

    def greet(i, carry):
        pl.semaphore_signal(
            barrier, inc=1, device_id=((e + i) % COLS, d), device_id_type=pl.DeviceIdType.MESH
        )
        return carry

    lax.fori_loop(1, COLS, greet, 0)
    for peer in (xp, xm, mate):
        pl.semaphore_signal(
            barrier, inc=1, device_id=(e, peer), device_id_type=pl.DeviceIdType.MESH
        )

    db[64:128, :] = jnp.zeros((64, DF), BF)

    hot = plc[0]
    is_hot = (hot == e).astype(F32)
    lane = lax.broadcasted_iota(jnp.int32, (TOK, LANE), 1)
    member = jnp.zeros((TOK, LANE), F32)
    weight = jnp.zeros((TOK, LANE), F32)
    for k in range(ids.shape[1]):
        same = ids[:, k : k + 1] == lane
        member = member + jnp.where(same, 1.0, 0.0)
        weight = weight + jnp.where(same, rw[:, k : k + 1], 0.0)
    row_i = lax.broadcasted_iota(jnp.int32, (TOK, TOK), 0)
    col_i = lax.broadcasted_iota(jnp.int32, (TOK, TOK), 1)
    before = jnp.where(row_i > col_i, 1.0, 0.0).astype(BF)
    rank = dot(before, member.astype(BF))
    hot_lane = jnp.where(lane == hot, 1.0, 0.0)
    cold = member * (1.0 - hot_lane)
    tokens = tok[...]
    grads = grad[...]
    ones = jnp.ones((TOK, DF), F32)
    for r in range(2):
        pick = jnp.where(rank == r, cold, 0.0)
        route[r] = pick
        route[2 + r] = pick * weight
        xr = t_dot(pick.astype(BF), tokens)
        gr = t_dot(pick.astype(BF), grads)
        wr = lax.dot_general(
            pick * weight, ones, (((0,), (0,)), ((), ())),
            precision=lax.Precision.HIGHEST, preferred_element_type=F32,
        )
        for q in range(4):
            cut = slice(q * LANE, (q + 1) * LANE)
            stage[pl.ds(r * 4 + q, COLS, stride=16), :] = xr[:COLS, cut]
            stage[pl.ds(8 + r * 4 + q, COLS, stride=16), :] = gr[:COLS, cut] * wr[:COLS, cut]
    nsend[...] = stage[...].astype(BF).reshape(COLS, 16, LANE)

    hm = jnp.sum(member * hot_lane, axis=1, keepdims=True)
    hw = jnp.sum(weight * hot_lane, axis=1, keepdims=True)
    hr = jnp.sum(rank * hot_lane, axis=1, keepdims=True)
    hpick = jnp.where(lane.astype(F32) == hr, hm, 0.0)
    hroute[0] = hpick
    hroute[1] = hpick * hw
    hx = t_dot(hpick.astype(BF), tokens)[0:8]
    hgr = t_dot(hpick.astype(BF), (hw * grads.astype(F32)).astype(BF))[0:8]
    count = jnp.broadcast_to(jnp.sum(member, axis=0, keepdims=True), (16, LANE))
    hg[z, y, :, 0:DF] = jnp.concatenate([hx, hgr], axis=0).astype(BF)
    hg[z, y, :, DF:HW] = count.astype(BF)

    pl.semaphore_wait(barrier, COLS - 1 + 3)

    for o in range(1, NY):
        push(hg.at[z, y], hg.at[z, y], s_y, r_y, (z * NY + (y + o) % NY, d))

    def send_n(i, carry):
        to = (e + i) % COLS
        push(nsend.at[to], nrecv.at[e], s_n, r_n, (to, d))
        return carry

    lax.fori_loop(1, COLS, send_n, 0)
    nrecv[e] = nsend[e]
    zp = ((z + 1) % NZ) * NY + y
    zm = ((z + NZ - 1) % NZ) * NY + y

    def ring_send(s):
        at = (z + NZ - s) % NZ
        push(hg.at[at], hg.at[at], s_zp.at[s], r_zp.at[s], (zp, d))

        @pl.when(s < 3)
        def _():
            am = (z + s) % NZ
            push(hg.at[am], hg.at[am], s_zm.at[s], r_zm.at[s], (zm, d))

    wait(hg.at[z, pl.ds(0, NY - 1)], r_y)
    ring_send(0)
    for load in loads:
        load.wait()

    def offset(p, i):
        first = p % 4 + 1
        return first if i == 0 else (8 - first) - 4 * (first // 4)

    def partial(p):
        xv = xs[p]
        gv = gs[p]

        def one(n, carry):
            at = pl.ds(pl.multiple_of(n * 512, 512), 512)
            pt[p, :, at] = dot(xv, gu[:, at]).astype(BF)
            return carry

        lax.fori_loop(0, 4, one, 0)
        pt[p, :, C_LOW:C_BACK] = dot(xv, ga[...]).astype(BF)
        for n in range(2):
            pt[p, :, C_BACK + n * 512 : C_BACK + (n + 1) * 512] = dot_t(
                gv, dn[n * 512 : (n + 1) * 512, :]
            ).astype(BF)
        pt[p, :, C_BL:WP] = dot_t(gv, db[...]).astype(BF)
        push(
            pt.at[p, pl.ds(pl.multiple_of((1 - c) * 64, 64), 64)], pr.at[p],
            s_pair.at[p], r_pair.at[p], (e, mate),
        )

    def rows_of(xx):
        return pl.ds(pl.multiple_of((xx % NX) * BLK, BLK), BLK)

    def block_of(core, xx):
        return pl.ds(pl.multiple_of((core * NX + xx % NX) * BLK, BLK), BLK)

    def tick(t, carry):
        @pl.when((t >= 6) & (t < 6 + PARTS))
        def _():
            p = t - 6
            wait(ag.at[p, pl.ds(0, 64)], r_core.at[p])
            hid = ag[p, :, 0:HID]
            hb = ag[p, :, A_HB:WA]
            out = dot(hid, dn[...]) + SCALE * dot(hb, db[...])
            both = ag[p, :, A_GB:A_LB]
            lb = ag[p, :, A_LB:A_LOW]
            dx = dot_t(both, gu[...]) + SCALE * dot_t(lb, ga[...])

            @pl.when(p == 0)
            def _():
                for r in range(2):
                    for q in range(4):
                        cut = slice(q * LANE, (q + 1) * LANE)
                        rs = slice(r * COLS, (r + 1) * COLS)
                        stage[pl.ds(r * 4 + q, COLS, stride=16), :] = out[rs, cut]
                        stage[pl.ds(8 + r * 4 + q, COLS, stride=16), :] = dx[rs, cut]
                nback[...] = stage[...].astype(BF).reshape(COLS, 16, LANE)

                def send_b(i, carry):
                    to = (e + i) % COLS
                    push(nback.at[to], nret.at[e], s_b, r_b, (to, d))
                    return carry

                lax.fori_loop(1, COLS, send_b, 0)
                nret[e] = nback[e]

            @pl.when(p > 0)
            def _():
                for i in range(2):
                    o = offset(p, i)
                    rs = slice(i * 64, (i + 1) * 64)
                    block = jnp.concatenate(
                        [out[rs].reshape(NY, 8, DF), dx[rs].reshape(NY, 8, DF)], axis=1
                    )
                    hret[o] = block.astype(BF)

                    @pl.when(o > 0)
                    def _():
                        push(
                            hret.at[o], hgot.at[o], s_h, r_h.at[o],
                            (((z + o) % NZ) * NY + y, d),
                        )

        @pl.when((t >= 5) & (t < 5 + PARTS))
        def _():
            p = t - 5
            far = block_of(c, x + 2)
            wait(ag.at[p, far, pl.ds(0, AHALF)], r_fwd.at[p, 0])
            wait(ag.at[p, far, pl.ds(AHALF, WA - AHALF)], r_fwd.at[p, 1])
            push(ag.at[p, far], ag.at[p, far], s_core.at[p], r_core.at[p], (e, mate))

        @pl.when((t >= 4) & (t < 4 + PARTS))
        def _():
            p = t - 4
            left = block_of(c, x + NX - 1)
            right = block_of(c, x + 1)
            lo = pl.ds(0, AHALF)
            hi = pl.ds(AHALF, WA - AHALF)
            wait(ag.at[p, left], r_agx.at[p, 0])
            push(ag.at[p, left, lo], ag.at[p, left, lo], s_ag.at[p], r_fwd.at[p, 0], (e, xp))
            push(ag.at[p, left], ag.at[p, left], s_core.at[p], r_core.at[p], (e, mate))
            wait(ag.at[p, right], r_agx.at[p, 1])
            push(ag.at[p, right, hi], ag.at[p, right, hi], s_ag.at[p], r_fwd.at[p, 1], (e, xm))
            push(ag.at[p, right], ag.at[p, right], s_core.at[p], r_core.at[p], (e, mate))

        @pl.when((t >= 3) & (t < 3 + PARTS))
        def _():
            p = t - 3
            wait(rb.at[p, 0], r_2b.at[p, 0])
            wait(rb.at[p, 1], r_2b.at[p, 1])
            own = rows_of(x)

            def total(lo, hi):
                return (
                    ss[p, own, lo:hi].astype(F32)
                    + rb[p, 0, :, lo:hi].astype(F32)
                    + rb[p, 1, :, lo:hi].astype(F32)
                )

            low = total(C_LOW, C_BACK).astype(BF)
            bl = total(C_BL, WP).astype(BF)
            left_half = lax.broadcasted_iota(jnp.int32, (BLK, LANE), 1) < 64
            low32 = low.astype(F32)
            low_g = jnp.where(left_half, low32, 0.0).astype(BF)
            low_u = jnp.where(left_half, 0.0, low32).astype(BF)
            gate = total(0, HID) + SCALE * dot(low_g, gb[...])
            up = total(HID, C_LOW) + SCALE * dot(low_u, gb[...])
            gh = total(C_BACK, C_BL) + SCALE * dot_t(bl[:, 0:64], da[...])
            sig = jax.nn.sigmoid(gate)
            act = gate * sig
            hidden = (act * up).astype(BF)
            gg = (gh * up * sig * (1.0 + gate * (1.0 - sig))).astype(BF)
            gup = (gh * act).astype(BF)
            hl = dot(hidden, da[...])
            lb = jnp.where(left_half, dot_t(gg, gb[...]), dot_t(gup, gb[...]))
            mine = block_of(c, x)
            ag[p, mine, 0:HID] = hidden
            ag[p, mine, HID : 2 * HID] = gg
            ag[p, mine, 2 * HID : A_LB] = gup
            ag[p, mine, A_LB:A_LOW] = lb.astype(BF)
            ag[p, mine, A_LOW:A_HB] = low
            ag[p, mine, A_HB:WA] = jnp.concatenate(
                [hl, bl[:, 0:64].astype(F32)], axis=1
            ).astype(BF)
            here = ag.at[p, mine]
            push(here, here, s_ag.at[p], r_agx.at[p, 0], (e, xp))
            push(here, here, s_ag.at[p], r_agx.at[p, 1], (e, xm))
            push(here, here, s_core.at[p], r_core.at[p], (e, mate))

        @pl.when((t >= 2) & (t < 2 + PARTS))
        def _():
            p = t - 2
            right = rows_of(x + 1)
            left = rows_of(x + NX - 1)
            wait(ra.at[p, 0], r_2a.at[p, 0])
            ss[p, right, 0:HALF] = (
                ss[p, right, 0:HALF].astype(F32) + ra[p, 0].astype(F32)
            ).astype(BF)
            push(ss.at[p, right], rb.at[p, 0], s_rs.at[p], r_2b.at[p, 0], (e, xp))
            wait(ra.at[p, 1], r_2a.at[p, 1])
            ss[p, left, HALF:WP] = (
                ss[p, left, HALF:WP].astype(F32) + ra[p, 1].astype(F32)
            ).astype(BF)
            push(ss.at[p, left], rb.at[p, 1], s_rs.at[p], r_2b.at[p, 1], (e, xm))

        @pl.when((t >= 1) & (t < 1 + PARTS))
        def _():
            p = t - 1
            wait(pr.at[p], r_pair.at[p])

            def add(i, carry):
                xx = (x + 2 + i) % NX
                mine = block_of(c, xx)
                at = rows_of(xx)
                ss[p, at, :] = (pt[p, mine, :].astype(F32) + pr[p, at, :].astype(F32)).astype(BF)

                @pl.when(i == 0)
                def _():
                    push(
                        ss.at[p, at, pl.ds(0, HALF)], ra.at[p, 0],
                        s_rs.at[p], r_2a.at[p, 0], (e, xp),
                    )
                    push(
                        ss.at[p, at, pl.ds(HALF, HALF)], ra.at[p, 1],
                        s_rs.at[p], r_2a.at[p, 1], (e, xm),
                    )

                return carry

            lax.fori_loop(0, NX, add, 0)

        @pl.when(t == 0)
        def _():
            wait(nrecv.at[pl.ds(0, COLS - 1)], r_n)
            stage[...] = nrecv[...].reshape(COLS * 16, LANE).astype(F32)
            for r in range(2):
                for q in range(4):
                    cut = slice(q * LANE, (q + 1) * LANE)
                    rs = slice(r * COLS, (r + 1) * COLS)
                    xs[0, rs, cut] = stage[pl.ds(r * 4 + q, COLS, stride=16), :].astype(BF)
                    gs[0, rs, cut] = stage[pl.ds(8 + r * 4 + q, COLS, stride=16), :].astype(BF)

        @pl.when(t < 4)
        def _():
            wait(hg.at[0], r_zp.at[t])

            @pl.when(t < 3)
            def _():
                wait(hg.at[0], r_zm.at[t])
                ring_send(t + 1)

        @pl.when((t >= 1) & (t < PARTS))
        def _():
            for i in range(2):
                plane = (z + offset(t, i)) % NZ
                v = hg[plane, :, :, 0:DF].astype(F32) * is_hot
                rs = slice(i * 64, (i + 1) * 64)
                xs[t, rs, :] = v[:, 0:8, :].reshape(64, DF).astype(BF)
                gs[t, rs, :] = v[:, 8:16, :].reshape(64, DF).astype(BF)

        @pl.when(t < PARTS)
        def _():
            partial(t)

        return carry

    lax.fori_loop(0, TICKS, tick, 0)

    for o in range(1, NZ):
        wait(hgot.at[o], r_h.at[o])
    got = hret[0].astype(F32)
    for o in range(1, NZ):
        got = got + hgot[o].astype(F32)
    ysend[...] = got.astype(BF)
    for o in range(1, NY):
        to = (y + o) % NY
        push(ysend.at[to], ygot.at[o], s_w, r_w, (z * NY + to, d))
    ygot[0] = ysend[y]

    xall = xs[...].reshape(PARTS * ROWS, DF)
    gall = gs[...].reshape(PARTS * ROWS, DF)

    def cols(lo, hi):
        return ag[:, :, lo:hi].reshape(PARTS * ROWS, hi - lo)

    gga_o[...] = SCALE * t_dot(cols(A_LB, A_LOW), xall).T
    hb = cols(A_HB, WA)
    low = cols(A_LOW, A_HB)
    ggb_o[0:64, :] = SCALE * t_dot(low, cols(A_GB, A_GB + HID))[0:64]
    ggb_o[64:128, :] = SCALE * t_dot(low, cols(A_GB + HID, A_LB))[64:128]
    gda_o[...] = SCALE * t_dot(hb, cols(0, HID))[64:128].T
    gdb_o[...] = SCALE * t_dot(hb, gall)[0:64]

    total = jnp.sum(
        hg[:, :, :, DF:HW].astype(F32).reshape(COLS * 16, LANE), axis=0, keepdims=True
    )
    lane1 = lax.broadcasted_iota(jnp.int32, (1, LANE), 1)
    mine = jnp.sum(jnp.where(lane1 == e, total, 0.0)) * (1.0 / 16.0)
    held = (plc[0] == e) | (plc[1] == e) | (plc[2] == e) | (plc[3] == e)
    share = COLS // 4 * 8
    rows = jnp.where(hot == e, 0, mine.astype(jnp.int32)) + jnp.where(held, share, 0)
    rows_o[0] = rows
    blocks_o[0] = (rows + 127) // 128

    wait(nret.at[pl.ds(0, COLS - 1)], r_b)
    stage[...] = nret[...].reshape(COLS * 16, LANE).astype(F32)
    wait(ygot.at[pl.ds(1, NY - 1)], r_w)
    back = ygot[0].astype(F32)
    for o in range(1, NY):
        back = back + ygot[o].astype(F32)

    def exact(a, b):
        return jnp.dot(a, b, precision=lax.Precision.HIGHEST, preferred_element_type=F32)

    hpick = hroute[0][:, 0:8]
    hpw = hroute[1][:, 0:8]
    for q in range(4):
        cut = slice(q * LANE, (q + 1) * LANE)
        mix = exact(hpw, back[0:8, cut])
        gt = exact(hpick, back[8:16, cut])
        for r in range(2):
            mix = mix + exact(route[2 + r][:, 0:COLS], stage[pl.ds(r * 4 + q, COLS, stride=16), :])
            gt = gt + dot(
                route[r][:, 0:COLS].astype(BF),
                stage[pl.ds(8 + r * 4 + q, COLS, stride=16), :].astype(BF),
            )
        mixed_o[:, cut] = mix.astype(BF)
        gtok_o[:, cut] = gt.astype(BF)

    wait(nsend.at[pl.ds(0, COLS - 1)], s_n)
    wait(nback.at[pl.ds(0, COLS - 1)], s_b)
    wait(hg.at[0, pl.ds(0, NY - 1)], s_y)
    for s in range(4):
        wait(hg.at[0], s_zp.at[s])
    for s in range(3):
        wait(hg.at[0], s_zm.at[s])
    wait(hret.at[pl.ds(1, NZ - 1)], s_h)
    wait(ysend.at[pl.ds(0, NY - 1)], s_w)
    for p in range(PARTS):
        wait(pt.at[p, pl.ds(0, 64)], s_pair.at[p])
        wait(ss.at[p, pl.ds(0, 48)], s_rs.at[p])
        wait(ag.at[p, pl.ds(0, 48)], s_ag.at[p])
        wait(ag.at[p, pl.ds(0, 64)], s_core.at[p])


def per_device(
    tokens, expert_ids, route_weight, placement, gate_up_base, down_base, gate_up_a, gate_up_b,
    down_a, down_b, grad_mixed,
):
    vmem = pl.BlockSpec(memory_space=pltpu.VMEM)
    smem = pl.BlockSpec(memory_space=pltpu.SMEM)
    hbm = pl.BlockSpec(memory_space=pl.ANY)
    dma = pltpu.SemaphoreType.DMA
    out = pl.pallas_call(
        kernel,
        out_shape=(
            jax.ShapeDtypeStruct((TOK, DF), BF),
            jax.ShapeDtypeStruct((TOK, DF), BF),
            jax.ShapeDtypeStruct((DF, 128), F32),
            jax.ShapeDtypeStruct((128, HID), F32),
            jax.ShapeDtypeStruct((HID, 64), F32),
            jax.ShapeDtypeStruct((64, DF), F32),
            jax.ShapeDtypeStruct((1,), jnp.int32),
            jax.ShapeDtypeStruct((1,), jnp.int32),
        ),
        in_specs=[vmem] * 4 + [smem] + [hbm] * 6,
        out_specs=[vmem] * 6 + [smem] * 2,
        scratch_shapes=[
            pltpu.VMEM((DF, 2 * HID), BF),
            pltpu.VMEM((HID, DF), BF),
            pltpu.VMEM((DF, 128), BF),
            pltpu.VMEM((128, HID), BF),
            pltpu.VMEM((HID, 64), BF),
            pltpu.VMEM((128, DF), BF),
            dma((6,)),
            pltpu.VMEM((4, TOK, LANE), F32),
            pltpu.VMEM((2, TOK, LANE), F32),
            pltpu.VMEM((COLS * 16, LANE), F32),
            pltpu.VMEM((COLS, 16, LANE), BF),
            pltpu.VMEM((COLS, 16, LANE), BF),
            pltpu.VMEM((COLS, 16, LANE), BF),
            pltpu.VMEM((COLS, 16, LANE), BF),
            pltpu.VMEM((NZ, NY, 16, HW), BF),
            pltpu.VMEM((PARTS, ROWS, DF), BF),
            pltpu.VMEM((PARTS, ROWS, DF), BF),
            pltpu.VMEM((PARTS, ROWS, WP), BF),
            pltpu.VMEM((PARTS, 64, WP), BF),
            pltpu.VMEM((PARTS, 64, WP), BF),
            pltpu.VMEM((PARTS, 2, BLK, HALF), BF),
            pltpu.VMEM((PARTS, 2, BLK, WP), BF),
            pltpu.VMEM((PARTS, ROWS, WA), BF),
            pltpu.VMEM((NZ, NY, 16, DF), BF),
            pltpu.VMEM((NZ, NY, 16, DF), BF),
            pltpu.VMEM((NY, 16, DF), BF),
            pltpu.VMEM((NY, 16, DF), BF),
            dma, dma, dma, dma, dma, dma,
            dma((4,)), dma((4,)), dma((3,)), dma((3,)),
            dma, dma((NZ,)), dma, dma,
            dma((PARTS,)), dma((PARTS,)),
            dma((PARTS,)), dma((PARTS, 2)), dma((PARTS, 2)),
            dma((PARTS,)), dma((PARTS, 2)), dma((PARTS, 2)),
            dma((PARTS,)), dma((PARTS,)),
        ],
        compiler_params=pltpu.CompilerParams(
            collective_id=0, has_side_effects=True, vmem_limit_bytes=56 * 1024 * 1024
        ),
    )(
        tokens, expert_ids, route_weight, grad_mixed, placement, gate_up_base[0], down_base[0],
        gate_up_a[0], gate_up_b[0], down_a[0], down_b[0],
    )
    mixed, gtok, gga, ggb, gda, gdb, rows, blocks = out
    return mixed, gtok, gga[None], ggb[None], gda[None], gdb[None], rows, blocks


def solution(mesh):
    return jax.shard_map(
        per_device,
        mesh=mesh,
        in_specs=(
            P("expert", "dp"),
            P("expert", None),
            P("expert", None),
            P(),
            P("expert", "dp", None),
            P("expert", None, "dp"),
            P("expert", "dp", None),
            P("expert", None, None),
            P("expert", None, None),
            P("expert", None, "dp"),
            P("expert", "dp"),
        ),
        out_specs=(
            P("expert", "dp"),
            P("expert", "dp"),
            P("expert", "dp", None),
            P("expert", None, None),
            P("expert", None, None),
            P("expert", None, "dp"),
            P("expert"),
            P("expert"),
        ),
        check_vma=False,
    )
```

time: 247 us -> 120 us (0.49)
  waiting for transfers between devices: 110 us -> 0 us
  Pallas kernels: 0 us -> 100 us
  starting transfers between devices: 43.5 us -> 0 us
  blocking collectives: 31.7 us -> 0 us
  matrix products: 25.2 us -> 0 us
  between operations: 16.1 us -> 4.17 us
  other arithmetic: 9.64 us -> 0 us
  local copies, waits for them, and re-layouts: 10 us -> 13.3 us
    pallas_call x0 -> x1, Pallas kernels: none -> 100 us  [per_device(): pl.pallas_call(kernel, out_shape=(jax.ShapeDtypeStruct((TOK, DF), BF), ja...]
    psum x1 -> x0, waiting for transfers between devices: 70.8 us -> none  [expert_forward(): lax.psum(partial_value.astype(jnp.bfloat16), 'dp').astype(jnp.float32)]
    all_to_all x4 -> x0, starting transfers between devices: 43.4 us -> none  [the longest x2 21.8 us: collect(): lax.all_to_all(buffer, 'expert', split_axis=0, concat_axis=0, tiled=True)]
    all_to_all x4 -> x0, waiting for transfers between devices: 39.4 us -> none  [the longest x2 32.5 us: dispatch(): lax.all_to_all(buffer, 'expert', split_axis=0, concat_axis=0, tiled=True)]
    psum x1 -> x0, blocking collectives: 31.7 us -> none  [per_device(): all_counts = lax.psum(dest_counts, 'expert')]
    dot_general x19 -> x0, matrix products: 25.2 us -> none  [the longest x7 7.64 us: trailing_product(): lax.dot_general(left, right, (((1,), (1,)), ((), ())), preferred_element_...]
    unnamed x30 -> x11, local copies, waits for them, and re-layouts: 2.47 us -> 13.3 us
    gather x2 -> x0, local copies, waits for them, and re-layouts: 3.96 us -> none  [the longest x1 1.98 us: per_device(): returned[slot_target].reshape(token_count, topk_count, feature_width)]
  transfers between devices with their start and end apart: 5 -> 0, of which waited for: 4 -> 0; matrix products, arithmetic and copies ran while one was open for 9% -> 0% of each run, Pallas kernels for 0% -> 0%
where the time goes in v1:
time: 120 us; the launch traced here: 118 us
  Pallas kernels  100 us (83%)
  local copies, waits for them, and re-layouts  13.3 us (11%)
  between operations  4.17 us (3%)
    pallas_call x1, Pallas kernels, per_device(): pl.pallas_call(kernel, out_shape=(jax.ShapeDtypeStruct((TOK, DF), BF), ja...  100 us
    unnamed x11, local copies, waits for them, and re-layouts  13.3 us

profile of v1, /device:TPU:6, one launch (start us, length us, event | category | flops | bytes accessed | tf_op | source)
XLA Modules:
  0.0 117.6 jit_solution(17838202224456125680)
XLA Ops:
  0.6 1.4 %copy.20.ids = s32[16,8]{1,0:T(8,128)} copy(s32[16,8]{0,1:T(8,128)} %param.12) | data formatting | bytes 1024 | tf_op args[1]
  2.0 1.4 %copy.21.rw = f32[16,8]{1,0:T(8,128)} copy(f32[16,8]{0,1:T(8,128)} %param.13) | data formatting | bytes 1024 | tf_op args[2]
  3.3 1.7 %copy.19 = bf16[1,1024,64]{2,1,0:T(8,128)(2,1)} copy(bf16[1,1024,64]{1,2,0:T(8,128)(2,1)} %param.19) | data formatting | bytes 262144 | tf_op args[8]
  5.1 100.1 %shard_map.170 = (bf16[16,512]{1,0:T(8,128)(2,1)}, bf16[16,512]{1,0:T(8,128)(2,1)}, f32[512,128]{1,0:T(8,128)}, f32[128,1024]{1,0:T(8,128)}, f32[1024,64]{1,0:T(...) custom-call(bf16[16,512]{1,0:T(8,128)(2,1)} %tok.1, s32[16,8]{1,0:T(8,128)} %copy.20.ids, f32[16,8]{1,0:T(8,128)} %copy.21.rw, ...), custom_call_target="tpu_custom_call" | custom-call | tf_op jit(solution)/shard_map/pallas_call | solution.py:475
  105.2 0.0 copy-start
  105.2 2.0 %copy.22 = f32[1,1024,64]{1,2,0:T(8,128)} copy(f32[1,1024,64]{2,1,0:T(8,128)} %bitcast.13) | data formatting | bytes 524288
  107.2 1.3 %copy.30 = bf16[16,512]{1,0:T(8,128)(2,1)} copy(bf16[16,512]{1,0:T(8,128)(2,1)} %get-tuple-element.40) | data formatting | bytes 32768
  108.5 1.3 %copy.31 = bf16[16,512]{1,0:T(8,128)(2,1)} copy(bf16[16,512]{1,0:T(8,128)(2,1)} %get-tuple-element.41) | data formatting | bytes 32768
  109.8 1.7 %copy.32 = f32[1,512,128]{2,1,0:T(8,128)} copy(f32[1,512,128]{2,1,0:T(8,128)} %bitcast.16) | data formatting | bytes 524288
  111.5 1.9 %copy.33 = f32[1,128,1024]{2,1,0:T(8,128)} copy(f32[1,128,1024]{2,1,0:T(8,128)} %bitcast.14) | data formatting | bytes 1048576
  113.4 0.0 copy-done
  113.4 0.7 copy.34
Async XLA Ops:
  105.2 8.2 %copy-start = (f32[64,512]{1,0:T(8,128)S(1)}, f32[64,512]{1,0:T(8,128)}, u32[]{:S(2)}) copy-start(f32[64,512]{1,0:T(8,128)} %get-tuple-element.21) | copy-start | bytes 393220

commit v2 on v1

--- a/solution.py
+++ b/solution.py
@@ -13,7 +13,7 @@
 TOK = 16
 DF = 512
 HID = 1024
-PARTS = 5
+PARTS = 4
 ROWS = 128
 BLK = 16
 LANE = 128
@@ -21,7 +21,7 @@
 HALF = 1664
 A_GB, A_LB, A_LOW, A_HB, WA = 1024, 3072, 3200, 3328, 3456
 AHALF = 1792
-HW = 640
+CUT = 256
 TICKS = PARTS + 6
 
 
@@ -42,8 +42,9 @@
     mixed_o, gtok_o, gga_o, ggb_o, gda_o, gdb_o, rows_o, blocks_o,
     gu, dn, ga, gb, da, db, wsem,
     route, hroute, stage, nsend, nrecv, nback, nret, hg, xs, gs, pt, pr, ss, ra, rb, ag,
-    hret, hgot, ysend, ygot,
-    s_n, r_n, s_b, r_b, s_y, r_y, s_zp, r_zp, s_zm, r_zm, s_h, r_h, s_w, r_w,
+    hret, hgot_a, hgot_b, ysend, ygot, zsend, zgot,
+    cy, cz, s_n, r_n, s_b, r_b, s_y, r_y, s_zp, r_zp, s_zm, r_zm,
+    s_cy, r_cy, s_cz, r_cz, s_ha, r_ha, s_hb, r_hb, s_w, r_w, s_v, r_v,
     s_pair, r_pair, s_rs, r_2a, r_2b, s_ag, r_agx, r_fwd, s_core, r_core,
 ):
     e = lax.axis_index("expert")
@@ -59,6 +60,24 @@
 
     def wait(ref, sem):
         pltpu.make_async_copy(ref, ref, sem).wait()
+
+    xp = ((x + 1) % NX) * 2 + c
+    xm = ((x + NX - 1) % NX) * 2 + c
+    mate = x * 2 + (1 - c)
+
+    barrier = pltpu.get_barrier_semaphore()
+
+    def greet(i, carry):
+        pl.semaphore_signal(
+            barrier, inc=1, device_id=((e + i) % COLS, d), device_id_type=pl.DeviceIdType.MESH
+        )
+        return carry
+
+    lax.fori_loop(1, COLS, greet, 0)
+    for peer in (xp, xm, mate):
+        pl.semaphore_signal(
+            barrier, inc=1, device_id=(e, peer), device_id_type=pl.DeviceIdType.MESH
+        )
 
     loads = [
         pltpu.make_async_copy(src, dst, wsem.at[i])
@@ -69,76 +88,58 @@
     for load in loads:
         load.start()
 
-    xp = ((x + 1) % NX) * 2 + c
-    xm = ((x + NX - 1) % NX) * 2 + c
-    mate = x * 2 + (1 - c)
-
-    barrier = pltpu.get_barrier_semaphore()
-
-    def greet(i, carry):
-        pl.semaphore_signal(
-            barrier, inc=1, device_id=((e + i) % COLS, d), device_id_type=pl.DeviceIdType.MESH
-        )
-        return carry
-
-    lax.fori_loop(1, COLS, greet, 0)
-    for peer in (xp, xm, mate):
-        pl.semaphore_signal(
-            barrier, inc=1, device_id=(e, peer), device_id_type=pl.DeviceIdType.MESH
-        )
-
     db[64:128, :] = jnp.zeros((64, DF), BF)
 
     hot = plc[0]
     is_hot = (hot == e).astype(F32)
-    lane = lax.broadcasted_iota(jnp.int32, (TOK, LANE), 1)
-    member = jnp.zeros((TOK, LANE), F32)
-    weight = jnp.zeros((TOK, LANE), F32)
-    for k in range(ids.shape[1]):
-        same = ids[:, k : k + 1] == lane
+    expert = lax.broadcasted_iota(jnp.int32, (LANE, TOK), 0)
+    member = jnp.zeros((LANE, TOK), F32)
+    weight = jnp.zeros((LANE, TOK), F32)
+    for k in range(ids.shape[0]):
+        same = ids[k : k + 1, :] == expert
         member = member + jnp.where(same, 1.0, 0.0)
-        weight = weight + jnp.where(same, rw[:, k : k + 1], 0.0)
+        weight = weight + jnp.where(same, rw[k : k + 1, :], 0.0)
     row_i = lax.broadcasted_iota(jnp.int32, (TOK, TOK), 0)
     col_i = lax.broadcasted_iota(jnp.int32, (TOK, TOK), 1)
-    before = jnp.where(row_i > col_i, 1.0, 0.0).astype(BF)
-    rank = dot(before, member.astype(BF))
-    hot_lane = jnp.where(lane == hot, 1.0, 0.0)
-    cold = member * (1.0 - hot_lane)
+    before = jnp.where(row_i < col_i, 1.0, 0.0).astype(BF)
+    rank = dot(member.astype(BF), before)
+    hot_row = jnp.where(expert == hot, 1.0, 0.0)
+    cold = member * (1.0 - hot_row)
     tokens = tok[...]
     grads = grad[...]
-    ones = jnp.ones((TOK, DF), F32)
     for r in range(2):
-        pick = jnp.where(rank == r, cold, 0.0)
+        pick = jnp.where(rank == r, cold, 0.0)[0:COLS]
+        pw = pick * weight[0:COLS]
         route[r] = pick
-        route[2 + r] = pick * weight
-        xr = t_dot(pick.astype(BF), tokens)
-        gr = t_dot(pick.astype(BF), grads)
-        wr = lax.dot_general(
-            pick * weight, ones, (((0,), (0,)), ((), ())),
-            precision=lax.Precision.HIGHEST, preferred_element_type=F32,
-        )
+        route[2 + r] = pw
+        xr = dot(pick.astype(BF), tokens)
+        gr = dot(pick.astype(BF), grads) * jnp.sum(pw, axis=1, keepdims=True)
         for q in range(4):
             cut = slice(q * LANE, (q + 1) * LANE)
-            stage[pl.ds(r * 4 + q, COLS, stride=16), :] = xr[:COLS, cut]
-            stage[pl.ds(8 + r * 4 + q, COLS, stride=16), :] = gr[:COLS, cut] * wr[:COLS, cut]
+            stage[pl.ds(r * 4 + q, COLS, stride=16), :] = xr[:, cut]
+            stage[pl.ds(8 + r * 4 + q, COLS, stride=16), :] = gr[:, cut]
     nsend[...] = stage[...].astype(BF).reshape(COLS, 16, LANE)
 
-    hm = jnp.sum(member * hot_lane, axis=1, keepdims=True)
-    hw = jnp.sum(weight * hot_lane, axis=1, keepdims=True)
-    hr = jnp.sum(rank * hot_lane, axis=1, keepdims=True)
-    hpick = jnp.where(lane.astype(F32) == hr, hm, 0.0)
+    hm = jnp.sum(member * hot_row, axis=0, keepdims=True)
+    hw = jnp.sum(weight * hot_row, axis=0, keepdims=True)
+    hr = jnp.sum(rank * hot_row, axis=0, keepdims=True)
+    place = lax.broadcasted_iota(jnp.int32, (8, TOK), 0).astype(F32)
+    hpick = jnp.where(place == hr, hm, 0.0)
+    hpw = hpick * hw
     hroute[0] = hpick
-    hroute[1] = hpick * hw
-    hx = t_dot(hpick.astype(BF), tokens)[0:8]
-    hgr = t_dot(hpick.astype(BF), (hw * grads.astype(F32)).astype(BF))[0:8]
-    count = jnp.broadcast_to(jnp.sum(member, axis=0, keepdims=True), (16, LANE))
-    hg[z, y, :, 0:DF] = jnp.concatenate([hx, hgr], axis=0).astype(BF)
-    hg[z, y, :, DF:HW] = count.astype(BF)
+    hroute[1] = hpw
+    hx = dot(hpick.astype(BF), tokens)
+    hgr = dot(hpick.astype(BF), grads) * jnp.sum(hpw, axis=1, keepdims=True)
+    hg[z, y] = jnp.concatenate([hx, hgr], axis=0).astype(BF)
+    cy[0] = dot_t(jnp.ones((16, TOK), BF), member.astype(BF)).astype(BF)
 
     pl.semaphore_wait(barrier, COLS - 1 + 3)
 
+    lo, hi = pl.ds(0, CUT), pl.ds(CUT, DF - CUT)
     for o in range(1, NY):
         push(hg.at[z, y], hg.at[z, y], s_y, r_y, (z * NY + (y + o) % NY, d))
+    for o in range(1, NY):
+        push(cy.at[0], cy.at[o], s_cy, r_cy, (z * NY + (y + o) % NY, d))
 
     def send_n(i, carry):
         to = (e + i) % COLS
@@ -149,24 +150,45 @@
     nrecv[e] = nsend[e]
     zp = ((z + 1) % NZ) * NY + y
     zm = ((z + NZ - 1) % NZ) * NY + y
-
-    def ring_send(s):
-        at = (z + NZ - s) % NZ
-        push(hg.at[at], hg.at[at], s_zp.at[s], r_zp.at[s], (zp, d))
-
-        @pl.when(s < 3)
-        def _():
-            am = (z + s) % NZ
-            push(hg.at[am], hg.at[am], s_zm.at[s], r_zm.at[s], (zm, d))
+    rows16 = pl.ds(0, 16)
+
+    def plane_half(at, h):
+        return hg.at[at % NZ, pl.ds(0, NY), rows16, (lo, hi)[h]]
+
+    def ring_send(s, h):
+        up = plane_half(z + NZ - s, h)
+        push(up, up, s_zp.at[s, h], r_zp.at[s, h], (zp, d))
+        if s < 3:
+            down = plane_half(z + s, h)
+            push(down, down, s_zm.at[s, h], r_zm.at[s, h], (zm, d))
+
+    def ring_wait(s):
+        for h in range(2):
+            wait(plane_half(0, h), r_zp.at[s, h])
+            if s < 3:
+                wait(plane_half(0, h), r_zm.at[s, h])
+                ring_send(s + 1, h)
 
     wait(hg.at[z, pl.ds(0, NY - 1)], r_y)
-    ring_send(0)
+    ring_send(0, 0)
+    ring_send(0, 1)
+    wait(cy.at[pl.ds(0, NY - 1)], r_cy)
+    count = cy[0].astype(F32)
+    for o in range(1, NY):
+        count = count + cy[o].astype(F32)
+    cz[0] = count.astype(BF)
+    for o in range(1, NZ):
+        push(cz.at[0], cz.at[o], s_cz, r_cz, (((z + o) % NZ) * NY + y, d))
     for load in loads:
         load.wait()
 
     def offset(p, i):
-        first = p % 4 + 1
-        return first if i == 0 else (8 - first) - 4 * (first // 4)
+        first = (p + 2) * ((p + 2) // 3) - 3 * (p // 3)
+        return first if i == 0 else (9 - first) % NZ
+
+    def hot_rows(p, i):
+        v = hg[(z + offset(p, i)) % NZ].astype(F32) * is_hot
+        return v[:, 0:8, :].reshape(64, DF), v[:, 8:16, :].reshape(64, DF)
 
     def partial(p):
         xv = xs[p]
@@ -225,22 +247,26 @@
                 lax.fori_loop(1, COLS, send_b, 0)
                 nret[e] = nback[e]
 
-            @pl.when(p > 0)
-            def _():
-                for i in range(2):
-                    o = offset(p, i)
-                    rs = slice(i * 64, (i + 1) * 64)
-                    block = jnp.concatenate(
-                        [out[rs].reshape(NY, 8, DF), dx[rs].reshape(NY, 8, DF)], axis=1
+            for i in range(2):
+                o = offset(p, i)
+                rs = slice(i * 64, (i + 1) * 64)
+                block = jnp.concatenate(
+                    [out[rs].reshape(NY, 8, DF), dx[rs].reshape(NY, 8, DF)], axis=1
+                )
+                hret[o] = (block * is_hot).astype(BF)
+                for v in range(1, NY):
+                    to = (y + v) % NY
+                    push(
+                        hret.at[o, to, rows16, hi], hgot_b.at[o, v], s_hb, r_hb.at[o],
+                        (z * NY + to, d),
                     )
-                    hret[o] = block.astype(BF)
-
-                    @pl.when(o > 0)
-                    def _():
-                        push(
-                            hret.at[o], hgot.at[o], s_h, r_h.at[o],
-                            (((z + o) % NZ) * NY + y, d),
-                        )
+
+                @pl.when(o > 0)
+                def _():
+                    push(
+                        hret.at[o, pl.ds(0, NY), rows16, lo], hgot_a.at[o], s_ha, r_ha.at[o],
+                        (((z + o) % NZ) * NY + y, d),
+                    )
 
         @pl.when((t >= 5) & (t < 5 + PARTS))
         def _():
@@ -286,13 +312,13 @@
             low_u = jnp.where(left_half, 0.0, low32).astype(BF)
             gate = total(0, HID) + SCALE * dot(low_g, gb[...])
             up = total(HID, C_LOW) + SCALE * dot(low_u, gb[...])
-            gh = total(C_BACK, C_BL) + SCALE * dot_t(bl[:, 0:64], da[...])
+            gh = total(C_BACK, C_BL) + SCALE * dot(bl[:, 0:64], da[...])
             sig = jax.nn.sigmoid(gate)
             act = gate * sig
             hidden = (act * up).astype(BF)
             gg = (gh * up * sig * (1.0 + gate * (1.0 - sig))).astype(BF)
             gup = (gh * act).astype(BF)
-            hl = dot(hidden, da[...])
+            hl = dot_t(hidden, da[...])
             lb = jnp.where(left_half, dot_t(gg, gb[...]), dot_t(gup, gb[...]))
             mine = block_of(c, x)
             ag[p, mine, 0:HID] = hidden
@@ -352,6 +378,7 @@
 
         @pl.when(t == 0)
         def _():
+            ring_wait(0)
             wait(nrecv.at[pl.ds(0, COLS - 1)], r_n)
             stage[...] = nrecv[...].reshape(COLS * 16, LANE).astype(F32)
             for r in range(2):
@@ -361,23 +388,28 @@
                     xs[0, rs, cut] = stage[pl.ds(r * 4 + q, COLS, stride=16), :].astype(BF)
                     gs[0, rs, cut] = stage[pl.ds(8 + r * 4 + q, COLS, stride=16), :].astype(BF)
 
-        @pl.when(t < 4)
-        def _():
-            wait(hg.at[0], r_zp.at[t])
-
-            @pl.when(t < 3)
-            def _():
-                wait(hg.at[0], r_zm.at[t])
-                ring_send(t + 1)
+            for i in range(2):
+                xv, gv = hot_rows(0, i)
+                rs = slice(i * 64, (i + 1) * 64)
+                xs[0, rs, :] = (xs[0, rs, :].astype(F32) + xv).astype(BF)
+                gs[0, rs, :] = (gs[0, rs, :].astype(F32) + gv).astype(BF)
+
+        @pl.when(t == 1)
+        def _():
+            ring_wait(1)
+            ring_wait(2)
+
+        @pl.when(t == 2)
+        def _():
+            ring_wait(3)
 
         @pl.when((t >= 1) & (t < PARTS))
         def _():
             for i in range(2):
-                plane = (z + offset(t, i)) % NZ
-                v = hg[plane, :, :, 0:DF].astype(F32) * is_hot
+                xv, gv = hot_rows(t, i)
                 rs = slice(i * 64, (i + 1) * 64)
-                xs[t, rs, :] = v[:, 0:8, :].reshape(64, DF).astype(BF)
-                gs[t, rs, :] = v[:, 8:16, :].reshape(64, DF).astype(BF)
+                xs[t, rs, :] = xv.astype(BF)
+                gs[t, rs, :] = gv.astype(BF)
 
         @pl.when(t < PARTS)
         def _():
@@ -388,15 +420,24 @@
     lax.fori_loop(0, TICKS, tick, 0)
 
     for o in range(1, NZ):
-        wait(hgot.at[o], r_h.at[o])
-    got = hret[0].astype(F32)
+        wait(hgot_a.at[o], r_ha.at[o])
+    got = hret[0, :, :, 0:CUT].astype(F32)
     for o in range(1, NZ):
-        got = got + hgot[o].astype(F32)
+        got = got + hgot_a[o].astype(F32)
     ysend[...] = got.astype(BF)
-    for o in range(1, NY):
-        to = (y + o) % NY
-        push(ysend.at[to], ygot.at[o], s_w, r_w, (z * NY + to, d))
+    for v in range(1, NY):
+        to = (y + v) % NY
+        push(ysend.at[to], ygot.at[v], s_w, r_w, (z * NY + to, d))
+    for o in range(NZ):
+        wait(hgot_b.at[o, pl.ds(0, NY - 1)], r_hb.at[o])
+        got = hret[o, y, :, CUT:DF].astype(F32)
+        for v in range(1, NY):
+            got = got + hgot_b[o, v].astype(F32)
+        zsend[o] = got.astype(BF)
+        if o > 0:
+            push(zsend.at[o], zgot.at[o], s_v, r_v, (((z + o) % NZ) * NY + y, d))
     ygot[0] = ysend[y]
+    zgot[0] = zsend[0]
 
     xall = xs[...].reshape(PARTS * ROWS, DF)
     gall = gs[...].reshape(PARTS * ROWS, DF)
@@ -409,12 +450,11 @@
     low = cols(A_LOW, A_HB)
     ggb_o[0:64, :] = SCALE * t_dot(low, cols(A_GB, A_GB + HID))[0:64]
     ggb_o[64:128, :] = SCALE * t_dot(low, cols(A_GB + HID, A_LB))[64:128]
-    gda_o[...] = SCALE * t_dot(hb, cols(0, HID))[64:128].T
+    gda_o[...] = SCALE * t_dot(hb, cols(0, HID))[64:128]
     gdb_o[...] = SCALE * t_dot(hb, gall)[0:64]
 
-    total = jnp.sum(
-        hg[:, :, :, DF:HW].astype(F32).reshape(COLS * 16, LANE), axis=0, keepdims=True
-    )
+    wait(cz.at[pl.ds(0, NZ - 1)], r_cz)
+    total = jnp.sum(cz[...].astype(F32).reshape(NZ * 16, LANE), axis=0, keepdims=True)
     lane1 = lax.broadcasted_iota(jnp.int32, (1, LANE), 1)
     mine = jnp.sum(jnp.where(lane1 == e, total, 0.0)) * (1.0 / 16.0)
     held = (plc[0] == e) | (plc[1] == e) | (plc[2] == e) | (plc[3] == e)
@@ -426,42 +466,66 @@
     wait(nret.at[pl.ds(0, COLS - 1)], r_b)
     stage[...] = nret[...].reshape(COLS * 16, LANE).astype(F32)
     wait(ygot.at[pl.ds(1, NY - 1)], r_w)
-    back = ygot[0].astype(F32)
+    wait(zgot.at[pl.ds(1, NZ - 1)], r_v)
+    back = [ygot[0].astype(F32), zgot[0].astype(F32)]
     for o in range(1, NY):
-        back = back + ygot[o].astype(F32)
+        back[0] = back[0] + ygot[o].astype(F32)
+        back[1] = back[1] + zgot[o].astype(F32)
 
     def exact(a, b):
-        return jnp.dot(a, b, precision=lax.Precision.HIGHEST, preferred_element_type=F32)
-
-    hpick = hroute[0][:, 0:8]
-    hpw = hroute[1][:, 0:8]
+        return lax.dot_general(
+            a, b, (((0,), (0,)), ((), ())),
+            precision=lax.Precision.HIGHEST, preferred_element_type=F32,
+        )
+
     for q in range(4):
         cut = slice(q * LANE, (q + 1) * LANE)
-        mix = exact(hpw, back[0:8, cut])
-        gt = exact(hpick, back[8:16, cut])
+        half = back[q // 2][:, (q % 2) * LANE : (q % 2 + 1) * LANE]
+        mix = exact(hroute[1], half[0:8])
+        gt = exact(hroute[0], half[8:16])
         for r in range(2):
-            mix = mix + exact(route[2 + r][:, 0:COLS], stage[pl.ds(r * 4 + q, COLS, stride=16), :])
-            gt = gt + dot(
-                route[r][:, 0:COLS].astype(BF),
-                stage[pl.ds(8 + r * 4 + q, COLS, stride=16), :].astype(BF),
+            mix = mix + exact(route[2 + r], stage[pl.ds(r * 4 + q, COLS, stride=16), :])
+            gt = gt + t_dot(
+                route[r].astype(BF), stage[pl.ds(8 + r * 4 + q, COLS, stride=16), :].astype(BF)
             )
         mixed_o[:, cut] = mix.astype(BF)
         gtok_o[:, cut] = gt.astype(BF)
 
     wait(nsend.at[pl.ds(0, COLS - 1)], s_n)
     wait(nback.at[pl.ds(0, COLS - 1)], s_b)
-    wait(hg.at[0, pl.ds(0, NY - 1)], s_y)
-    for s in range(4):
-        wait(hg.at[0], s_zp.at[s])
-    for s in range(3):
-        wait(hg.at[0], s_zm.at[s])
-    wait(hret.at[pl.ds(1, NZ - 1)], s_h)
+    wait(hg.at[z, pl.ds(0, NY - 1)], s_y)
+    for h in range(2):
+        for s in range(4):
+            wait(plane_half(0, h), s_zp.at[s, h])
+        for s in range(3):
+            wait(plane_half(0, h), s_zm.at[s, h])
+    wait(cy.at[pl.ds(0, NY - 1)], s_cy)
+    wait(cz.at[pl.ds(0, NZ - 1)], s_cz)
+    wait(hgot_a.at[pl.ds(1, NZ - 1)], s_ha)
+    wait(hgot_b.at[pl.ds(0, NZ), pl.ds(0, NY - 1)], s_hb)
     wait(ysend.at[pl.ds(0, NY - 1)], s_w)
+    wait(zsend.at[pl.ds(0, NZ - 1)], s_v)
     for p in range(PARTS):
         wait(pt.at[p, pl.ds(0, 64)], s_pair.at[p])
         wait(ss.at[p, pl.ds(0, 48)], s_rs.at[p])
         wait(ag.at[p, pl.ds(0, 48)], s_ag.at[p])
         wait(ag.at[p, pl.ds(0, 64)], s_core.at[p])
+
+
+def copy_kernel(*refs):
+    n = len(refs) // 2
+    for i in range(n):
+        refs[n + i][...] = refs[i][...]
+
+
+def hand_over(arrays):
+    vmem = pl.BlockSpec(memory_space=pltpu.VMEM)
+    return pl.pallas_call(
+        copy_kernel,
+        out_shape=tuple(jax.ShapeDtypeStruct(a.shape, a.dtype) for a in arrays),
+        in_specs=[vmem] * len(arrays),
+        out_specs=tuple([vmem] * len(arrays)),
+    )(*arrays)
 
 
 def per_device(
@@ -479,7 +543,7 @@
             jax.ShapeDtypeStruct((TOK, DF), BF),
             jax.ShapeDtypeStruct((DF, 128), F32),
             jax.ShapeDtypeStruct((128, HID), F32),
-            jax.ShapeDtypeStruct((HID, 64), F32),
+            jax.ShapeDtypeStruct((64, HID), F32),
             jax.ShapeDtypeStruct((64, DF), F32),
             jax.ShapeDtypeStruct((1,), jnp.int32),
             jax.ShapeDtypeStruct((1,), jnp.int32),
@@ -491,17 +555,17 @@
             pltpu.VMEM((HID, DF), BF),
             pltpu.VMEM((DF, 128), BF),
             pltpu.VMEM((128, HID), BF),
-            pltpu.VMEM((HID, 64), BF),
+            pltpu.VMEM((64, HID), BF),
             pltpu.VMEM((128, DF), BF),
             dma((6,)),
-            pltpu.VMEM((4, TOK, LANE), F32),
-            pltpu.VMEM((2, TOK, LANE), F32),
+            pltpu.VMEM((4, COLS, TOK), F32),
+            pltpu.VMEM((2, 8, TOK), F32),
             pltpu.VMEM((COLS * 16, LANE), F32),
             pltpu.VMEM((COLS, 16, LANE), BF),
             pltpu.VMEM((COLS, 16, LANE), BF),
             pltpu.VMEM((COLS, 16, LANE), BF),
             pltpu.VMEM((COLS, 16, LANE), BF),
-            pltpu.VMEM((NZ, NY, 16, HW), BF),
+            pltpu.VMEM((NZ, NY, 16, DF), BF),
             pltpu.VMEM((PARTS, ROWS, DF), BF),
             pltpu.VMEM((PARTS, ROWS, DF), BF),
             pltpu.VMEM((PARTS, ROWS, WP), BF),
@@ -511,12 +575,18 @@
             pltpu.VMEM((PARTS, 2, BLK, WP), BF),
             pltpu.VMEM((PARTS, ROWS, WA), BF),
             pltpu.VMEM((NZ, NY, 16, DF), BF),
-            pltpu.VMEM((NZ, NY, 16, DF), BF),
-            pltpu.VMEM((NY, 16, DF), BF),
-            pltpu.VMEM((NY, 16, DF), BF),
+            pltpu.VMEM((NZ, NY, 16, CUT), BF),
+            pltpu.VMEM((NZ, NY, 16, DF - CUT), BF),
+            pltpu.VMEM((NY, 16, CUT), BF),
+            pltpu.VMEM((NY, 16, CUT), BF),
+            pltpu.VMEM((NZ, 16, DF - CUT), BF),
+            pltpu.VMEM((NZ, 16, DF - CUT), BF),
+            pltpu.VMEM((NY, 16, LANE), BF),
+            pltpu.VMEM((NZ, 16, LANE), BF),
             dma, dma, dma, dma, dma, dma,
-            dma((4,)), dma((4,)), dma((3,)), dma((3,)),
-            dma, dma((NZ,)), dma, dma,
+            dma((4, 2)), dma((4, 2)), dma((3, 2)), dma((3, 2)),
+            dma, dma, dma, dma,
+            dma, dma((NZ,)), dma, dma((NZ,)), dma, dma, dma, dma,
             dma((PARTS,)), dma((PARTS,)),
             dma((PARTS,)), dma((PARTS, 2)), dma((PARTS, 2)),
             dma((PARTS,)), dma((PARTS, 2)), dma((PARTS, 2)),
@@ -526,11 +596,11 @@
             collective_id=0, has_side_effects=True, vmem_limit_bytes=56 * 1024 * 1024
         ),
     )(
-        tokens, expert_ids, route_weight, grad_mixed, placement, gate_up_base[0], down_base[0],
-        gate_up_a[0], gate_up_b[0], down_a[0], down_b[0],
+        tokens, expert_ids.T, route_weight.T, grad_mixed, placement, gate_up_base[0], down_base[0],
+        gate_up_a[0], gate_up_b[0], down_a[0].T, down_b[0],
     )
-    mixed, gtok, gga, ggb, gda, gdb, rows, blocks = out
-    return mixed, gtok, gga[None], ggb[None], gda[None], gdb[None], rows, blocks
+    mixed, gtok, gga, ggb, gda, gdb = hand_over(out[:6])
+    return mixed, gtok, gga[None], ggb[None], gda.T[None], gdb[None], out[6], out[7]
 
 
 def solution(mesh):

time: 120 us -> 99.5 us (0.83)
  local copies, waits for them, and re-layouts: 13.3 us -> 0 us
  Pallas kernels: 100 us -> 93.8 us
    unnamed x11 -> x0, local copies, waits for them, and re-layouts: 13.3 us -> none
    pallas_call x1, Pallas kernels: 100 us -> 91.5 us  [per_device(): pl.pallas_call(kernel, out_shape=(jax.ShapeDtypeStruct((TOK, DF), BF), ja...]
    pallas_call x0 -> x1, Pallas kernels: none -> 2.3 us  [hand_over(): pl.pallas_call(copy_kernel, out_shape=tuple((jax.ShapeDtypeStruct(a.shape...]
where the time goes in v2:
time: 99.5 us; the launch traced here: 98 us
  Pallas kernels  93.8 us (94%)
  between operations  4.16 us (4%)
    pallas_call x1, Pallas kernels, per_device(): pl.pallas_call(kernel, out_shape=(jax.ShapeDtypeStruct((TOK, DF), BF), ja...  91.5 us
    pallas_call x1, Pallas kernels, hand_over(): pl.pallas_call(copy_kernel, out_shape=tuple((jax.ShapeDtypeStruct(a.shape...  2.3 us

profile of v2, /device:TPU:6, one launch (start us, length us, event | category | flops | bytes accessed | tf_op | source)
XLA Modules:
  0.0 98.0 jit_solution(10255502051589250230)
XLA Ops:
  0.6 91.5 %shard_map.170 = (bf16[16,512]{1,0:T(8,128)(2,1)}, bf16[16,512]{1,0:T(8,128)(2,1)}, f32[512,128]{1,0:T(8,128)}, f32[128,1024]{1,0:T(8,128)}, f32[64,1024]{1,0:T(...) custom-call(bf16[16,512]{1,0:T(8,128)(2,1)} %tok.1, s32[8,16]{1,0:T(8,128)} %bitcast.22, f32[8,16]{1,0:T(8,128)} %bitcast.23, ...), custom_call_target="tpu_custom_call" | custom-call | tf_op jit(solution)/shard_map/pallas_call | solution.py:539
  92.2 2.3 %shard_map.171 = (bf16[16,512]{1,0:T(8,128)(2,1)}, bf16[16,512]{1,0:T(8,128)(2,1)}, f32[512,128]{1,0:T(8,128)}, f32[128,1024]{1,0:T(8,128)}, f32[64,1024]{1,0:T(8,128)}, /*index=5*/f32[64,512]{1,0:T(8,128)}) custom-call(bf16[16,512]{1,0:T(8,128)(2,1)} %get-tuple-element.22.refs_0_, bf16[16,512]{1,0:T(8,128)(2,1)} %get-tuple-element.23.refs_1_, ...), custom_call_target="tpu_custom_call" | custom-call | tf_op jit(solution)/shard_map/pallas_call | solution.py:523

commit v3 on v2

--- a/solution.py
+++ b/solution.py
@@ -22,7 +22,8 @@
 A_GB, A_LB, A_LOW, A_HB, WA = 1024, 3072, 3200, 3328, 3456
 AHALF = 1792
 CUT = 256
-TICKS = PARTS + 6
+GAP, STEP = 1, 1
+TICKS = GAP * (PARTS - 1) + 6 * STEP + 1
 
 
 def dot(a, b):
@@ -41,9 +42,9 @@
     tok, ids, rw, grad, plc, gu_h, dn_h, ga_h, gb_h, da_h, db_h,
     mixed_o, gtok_o, gga_o, ggb_o, gda_o, gdb_o, rows_o, blocks_o,
     gu, dn, ga, gb, da, db, wsem,
-    route, hroute, stage, nsend, nrecv, nback, nret, hg, xs, gs, pt, pr, ss, ra, rb, ag,
+    route, hroute, stage, nsend, nmid, nrecv, nback, nhalf, nret, hg, xs, gs, pt, pr, ss, ra, rb, ag,
     hret, hgot_a, hgot_b, ysend, ygot, zsend, zgot,
-    cy, cz, s_n, r_n, s_b, r_b, s_y, r_y, s_zp, r_zp, s_zm, r_zm,
+    cy, cz, s_n, r_n, s_n2, r_n2, s_b, r_b, s_b2, r_b2, s_y, r_y, s_zp, r_zp, s_zm, r_zm,
     s_cy, r_cy, s_cz, r_cz, s_ha, r_ha, s_hb, r_hb, s_w, r_w, s_v, r_v,
     s_pair, r_pair, s_rs, r_2a, r_2b, s_ag, r_agx, r_fwd, s_core, r_core,
 ):
@@ -67,13 +68,11 @@
 
     barrier = pltpu.get_barrier_semaphore()
 
-    def greet(i, carry):
-        pl.semaphore_signal(
-            barrier, inc=1, device_id=((e + i) % COLS, d), device_id_type=pl.DeviceIdType.MESH
-        )
-        return carry
-
-    lax.fori_loop(1, COLS, greet, 0)
+    for o in range(1, NY):
+        for peer in (z * NY + (y + o) % NY, ((z + o) % NZ) * NY + y):
+            pl.semaphore_signal(
+                barrier, inc=1, device_id=(peer, d), device_id_type=pl.DeviceIdType.MESH
+            )
     for peer in (xp, xm, mate):
         pl.semaphore_signal(
             barrier, inc=1, device_id=(e, peer), device_id_type=pl.DeviceIdType.MESH
@@ -92,62 +91,70 @@
 
     hot = plc[0]
     is_hot = (hot == e).astype(F32)
-    expert = lax.broadcasted_iota(jnp.int32, (LANE, TOK), 0)
-    member = jnp.zeros((LANE, TOK), F32)
-    weight = jnp.zeros((LANE, TOK), F32)
-    for k in range(ids.shape[0]):
-        same = ids[k : k + 1, :] == expert
-        member = member + jnp.where(same, 1.0, 0.0)
-        weight = weight + jnp.where(same, rw[k : k + 1, :], 0.0)
     row_i = lax.broadcasted_iota(jnp.int32, (TOK, TOK), 0)
     col_i = lax.broadcasted_iota(jnp.int32, (TOK, TOK), 1)
     before = jnp.where(row_i < col_i, 1.0, 0.0).astype(BF)
-    rank = dot(member.astype(BF), before)
+
+    def membership(expert):
+        member = jnp.zeros(expert.shape, F32)
+        weight = jnp.zeros(expert.shape, F32)
+        for k in range(ids.shape[0]):
+            same = ids[k : k + 1, :] == expert
+            member = member + jnp.where(same, 1.0, 0.0)
+            weight = weight + jnp.where(same, rw[k : k + 1, :], 0.0)
+        return member, weight, dot(member.astype(BF), before)
+
+    expert = lax.broadcasted_iota(jnp.int32, (LANE, TOK), 0)
+    member, weight, rank = membership(expert)
     hot_row = jnp.where(expert == hot, 1.0, 0.0)
-    cold = member * (1.0 - hot_row)
     tokens = tok[...]
     grads = grad[...]
+    hm = jnp.sum(member * hot_row, axis=0, keepdims=True)
+    hw = jnp.sum(weight * hot_row, axis=0, keepdims=True)
+    hr = jnp.sum(rank * hot_row, axis=0, keepdims=True)
+    place = lax.broadcasted_iota(jnp.int32, (8, TOK), 0).astype(F32)
+    hpick = jnp.where(place == hr, hm, 0.0)
+    hpw = hpick * hw
+    hroute[0] = hpick.T
+    hroute[1] = hpw.T
+    hx = dot(hpick.astype(BF), tokens)
+    hgr = dot(hpick.astype(BF), grads) * jnp.sum(hpw, axis=1, keepdims=True)
+    hg[z, y] = jnp.concatenate([hx, hgr], axis=0).astype(BF)
+    cy[0] = dot_t(jnp.ones((16, TOK), BF), member.astype(BF)).astype(BF)
+
+    pl.semaphore_wait(barrier, NY - 1 + NZ - 1 + 3)
+
+    lo, hi = pl.ds(0, CUT), pl.ds(CUT, DF - CUT)
+    for o in range(1, NY):
+        push(hg.at[z, y], hg.at[z, y], s_y, r_y, (z * NY + (y + o) % NY, d))
+    for o in range(1, NY):
+        push(cy.at[0], cy.at[o], s_cy, r_cy, (z * NY + (y + o) % NY, d))
+
+    def keep(at, value):
+        head = value.astype(BF)
+        route[at] = head
+        route[at + 1] = (value - head.astype(F32)).astype(BF)
+
+    away = lax.broadcasted_iota(jnp.int32, (COLS, TOK), 0)
+    there = ((z + (away >> 3)) & (NZ - 1)) * NY + ((y + (away & 7)) & (NY - 1))
+    near, near_w, near_rank = membership(there)
+    cold = jnp.where(there == hot, 0.0, near)
     for r in range(2):
-        pick = jnp.where(rank == r, cold, 0.0)[0:COLS]
-        pw = pick * weight[0:COLS]
-        route[r] = pick
-        route[2 + r] = pw
+        pick = jnp.where(near_rank == r, cold, 0.0)
+        pw = pick * near_w
+        route[r] = pick.astype(BF)
+        keep(2 + 2 * r, pw)
         xr = dot(pick.astype(BF), tokens)
         gr = dot(pick.astype(BF), grads) * jnp.sum(pw, axis=1, keepdims=True)
         for q in range(4):
             cut = slice(q * LANE, (q + 1) * LANE)
             stage[pl.ds(r * 4 + q, COLS, stride=16), :] = xr[:, cut]
             stage[pl.ds(8 + r * 4 + q, COLS, stride=16), :] = gr[:, cut]
-    nsend[...] = stage[...].astype(BF).reshape(COLS, 16, LANE)
-
-    hm = jnp.sum(member * hot_row, axis=0, keepdims=True)
-    hw = jnp.sum(weight * hot_row, axis=0, keepdims=True)
-    hr = jnp.sum(rank * hot_row, axis=0, keepdims=True)
-    place = lax.broadcasted_iota(jnp.int32, (8, TOK), 0).astype(F32)
-    hpick = jnp.where(place == hr, hm, 0.0)
-    hpw = hpick * hw
-    hroute[0] = hpick
-    hroute[1] = hpw
-    hx = dot(hpick.astype(BF), tokens)
-    hgr = dot(hpick.astype(BF), grads) * jnp.sum(hpw, axis=1, keepdims=True)
-    hg[z, y] = jnp.concatenate([hx, hgr], axis=0).astype(BF)
-    cy[0] = dot_t(jnp.ones((16, TOK), BF), member.astype(BF)).astype(BF)
-
-    pl.semaphore_wait(barrier, COLS - 1 + 3)
-
-    lo, hi = pl.ds(0, CUT), pl.ds(CUT, DF - CUT)
-    for o in range(1, NY):
-        push(hg.at[z, y], hg.at[z, y], s_y, r_y, (z * NY + (y + o) % NY, d))
-    for o in range(1, NY):
-        push(cy.at[0], cy.at[o], s_cy, r_cy, (z * NY + (y + o) % NY, d))
-
-    def send_n(i, carry):
-        to = (e + i) % COLS
-        push(nsend.at[to], nrecv.at[e], s_n, r_n, (to, d))
-        return carry
-
-    lax.fori_loop(1, COLS, send_n, 0)
-    nrecv[e] = nsend[e]
+    nsend[...] = stage[...].astype(BF).reshape(NZ, NY, 16, LANE)
+    for o in range(1, NZ):
+        push(nsend.at[o], nmid.at[o], s_n, r_n, (((z + o) % NZ) * NY + y, d))
+    nmid[0] = nsend[0]
+
     zp = ((z + 1) % NZ) * NY + y
     zm = ((z + NZ - 1) % NZ) * NY + y
     rows16 = pl.ds(0, 16)
@@ -172,6 +179,14 @@
     wait(hg.at[z, pl.ds(0, NY - 1)], r_y)
     ring_send(0, 0)
     ring_send(0, 1)
+
+    wait(nmid.at[pl.ds(0, NZ - 1)], r_n)
+    for o in range(1, NY):
+        push(
+            nmid.at[pl.ds(0, NZ), o], nrecv.at[pl.ds(0, NZ), o], s_n2, r_n2,
+            (z * NY + (y + o) % NY, d),
+        )
+    nrecv[:, 0] = nmid[:, 0]
     wait(cy.at[pl.ds(0, NY - 1)], r_cy)
     count = cy[0].astype(F32)
     for o in range(1, NY):
@@ -217,10 +232,16 @@
     def block_of(core, xx):
         return pl.ds(pl.multiple_of((core * NX + xx % NX) * BLK, BLK), BLK)
 
+    def due(t, stage):
+        since = t - stage * STEP
+        return (since >= 0) & (since < GAP * PARTS) & ((since + 6 * STEP * GAP) % GAP == 0)
+
+    first, second = pl.ds(0, HALF), pl.ds(HALF, HALF)
+
     def tick(t, carry):
-        @pl.when((t >= 6) & (t < 6 + PARTS))
-        def _():
-            p = t - 6
+        @pl.when(due(t, 6))
+        def _():
+            p = (t - 6 * STEP) // GAP
             wait(ag.at[p, pl.ds(0, 64)], r_core.at[p])
             hid = ag[p, :, 0:HID]
             hb = ag[p, :, A_HB:WA]
@@ -229,7 +250,29 @@
             lb = ag[p, :, A_LB:A_LOW]
             dx = dot_t(both, gu[...]) + SCALE * dot_t(lb, ga[...])
 
-            @pl.when(p == 0)
+            for i in range(2):
+                o = offset(p, i)
+                rs = slice(i * 64, (i + 1) * 64)
+                block = jnp.concatenate(
+                    [out[rs].reshape(NY, 8, DF), dx[rs].reshape(NY, 8, DF)], axis=1
+                )
+                hret[p, i] = (block * is_hot).astype(BF)
+
+                @pl.when(o > 0)
+                def _():
+                    push(
+                        hret.at[p, i, pl.ds(0, NY), rows16, lo], hgot_a.at[o], s_ha, r_ha.at[o],
+                        (((z + o) % NZ) * NY + y, d),
+                    )
+
+            for v in range(1, NY):
+                to = (y + v) % NY
+                push(
+                    hret.at[p, pl.ds(0, 2), to, rows16, hi], hgot_b.at[p, v], s_hb, r_hb.at[p],
+                    (z * NY + to, d),
+                )
+
+            @pl.when(p == 1)
             def _():
                 for r in range(2):
                     for q in range(4):
@@ -237,48 +280,32 @@
                         rs = slice(r * COLS, (r + 1) * COLS)
                         stage[pl.ds(r * 4 + q, COLS, stride=16), :] = out[rs, cut]
                         stage[pl.ds(8 + r * 4 + q, COLS, stride=16), :] = dx[rs, cut]
-                nback[...] = stage[...].astype(BF).reshape(COLS, 16, LANE)
-
-                def send_b(i, carry):
-                    to = (e + i) % COLS
-                    push(nback.at[to], nret.at[e], s_b, r_b, (to, d))
-                    return carry
-
-                lax.fori_loop(1, COLS, send_b, 0)
-                nret[e] = nback[e]
-
-            for i in range(2):
-                o = offset(p, i)
-                rs = slice(i * 64, (i + 1) * 64)
-                block = jnp.concatenate(
-                    [out[rs].reshape(NY, 8, DF), dx[rs].reshape(NY, 8, DF)], axis=1
-                )
-                hret[o] = (block * is_hot).astype(BF)
+                nback[...] = stage[...].astype(BF).reshape(NZ, NY, 16, LANE)
                 for v in range(1, NY):
-                    to = (y + v) % NY
                     push(
-                        hret.at[o, to, rows16, hi], hgot_b.at[o, v], s_hb, r_hb.at[o],
-                        (z * NY + to, d),
+                        nback.at[pl.ds(0, NZ), v], nhalf.at[pl.ds(0, NZ), v], s_b, r_b,
+                        (z * NY + (y + NY - v) % NY, d),
                     )
-
-                @pl.when(o > 0)
-                def _():
-                    push(
-                        hret.at[o, pl.ds(0, NY), rows16, lo], hgot_a.at[o], s_ha, r_ha.at[o],
-                        (((z + o) % NZ) * NY + y, d),
-                    )
-
-        @pl.when((t >= 5) & (t < 5 + PARTS))
-        def _():
-            p = t - 5
+                nhalf[:, 0] = nback[:, 0]
+
+        @pl.when(t == GAP + 6 * STEP + 2)
+        def _():
+            wait(nhalf.at[pl.ds(0, NZ), pl.ds(0, NY - 1)], r_b)
+            for o in range(1, NZ):
+                push(nhalf.at[o], nret.at[o], s_b2, r_b2, (((z + NZ - o) % NZ) * NY + y, d))
+            nret[0] = nhalf[0]
+
+        @pl.when(due(t, 5))
+        def _():
+            p = (t - 5 * STEP) // GAP
             far = block_of(c, x + 2)
             wait(ag.at[p, far, pl.ds(0, AHALF)], r_fwd.at[p, 0])
             wait(ag.at[p, far, pl.ds(AHALF, WA - AHALF)], r_fwd.at[p, 1])
             push(ag.at[p, far], ag.at[p, far], s_core.at[p], r_core.at[p], (e, mate))
 
-        @pl.when((t >= 4) & (t < 4 + PARTS))
-        def _():
-            p = t - 4
+        @pl.when(due(t, 4))
+        def _():
+            p = (t - 4 * STEP) // GAP
             left = block_of(c, x + NX - 1)
             right = block_of(c, x + 1)
             lo = pl.ds(0, AHALF)
@@ -290,9 +317,9 @@
             push(ag.at[p, right, hi], ag.at[p, right, hi], s_ag.at[p], r_fwd.at[p, 1], (e, xm))
             push(ag.at[p, right], ag.at[p, right], s_core.at[p], r_core.at[p], (e, mate))
 
-        @pl.when((t >= 3) & (t < 3 + PARTS))
-        def _():
-            p = t - 3
+        @pl.when(due(t, 3))
+        def _():
+            p = (t - 3 * STEP) // GAP
             wait(rb.at[p, 0], r_2b.at[p, 0])
             wait(rb.at[p, 1], r_2b.at[p, 1])
             own = rows_of(x)
@@ -334,25 +361,31 @@
             push(here, here, s_ag.at[p], r_agx.at[p, 1], (e, xm))
             push(here, here, s_core.at[p], r_core.at[p], (e, mate))
 
-        @pl.when((t >= 2) & (t < 2 + PARTS))
-        def _():
-            p = t - 2
+        @pl.when(due(t, 2))
+        def _():
+            p = (t - 2 * STEP) // GAP
             right = rows_of(x + 1)
             left = rows_of(x + NX - 1)
             wait(ra.at[p, 0], r_2a.at[p, 0])
             ss[p, right, 0:HALF] = (
                 ss[p, right, 0:HALF].astype(F32) + ra[p, 0].astype(F32)
             ).astype(BF)
-            push(ss.at[p, right], rb.at[p, 0], s_rs.at[p], r_2b.at[p, 0], (e, xp))
+            push(
+                ss.at[p, right, first], rb.at[p, 0, rows16, first],
+                s_rs.at[p], r_2b.at[p, 0], (e, xp),
+            )
             wait(ra.at[p, 1], r_2a.at[p, 1])
             ss[p, left, HALF:WP] = (
                 ss[p, left, HALF:WP].astype(F32) + ra[p, 1].astype(F32)
             ).astype(BF)
-            push(ss.at[p, left], rb.at[p, 1], s_rs.at[p], r_2b.at[p, 1], (e, xm))
-
-        @pl.when((t >= 1) & (t < 1 + PARTS))
-        def _():
-            p = t - 1
+            push(
+                ss.at[p, left, second], rb.at[p, 1, rows16, second],
+                s_rs.at[p], r_2b.at[p, 1], (e, xm),
+            )
+
+        @pl.when(due(t, 1))
+        def _():
+            p = (t - 1 * STEP) // GAP
             wait(pr.at[p], r_pair.at[p])
 
             def add(i, carry):
@@ -375,83 +408,97 @@
                 return carry
 
             lax.fori_loop(0, NX, add, 0)
+            push(
+                ss.at[p, rows_of(x + 1), second], rb.at[p, 0, rows16, second],
+                s_rs.at[p], r_2b.at[p, 0], (e, xp),
+            )
+            push(
+                ss.at[p, rows_of(x + NX - 1), first], rb.at[p, 1, rows16, first],
+                s_rs.at[p], r_2b.at[p, 1], (e, xm),
+            )
 
         @pl.when(t == 0)
         def _():
             ring_wait(0)
-            wait(nrecv.at[pl.ds(0, COLS - 1)], r_n)
+
+        @pl.when(t == 1)
+        def _():
+            ring_wait(1)
+
+        @pl.when(t == GAP)
+        def _():
+            ring_wait(2)
+
+        @pl.when(t == 2 * GAP)
+        def _():
+            ring_wait(3)
+
+        @pl.when(due(t, 0))
+        def _():
+            p = t // GAP
+            for i in range(2):
+                xv, gv = hot_rows(p, i)
+                rs = slice(i * 64, (i + 1) * 64)
+                xs[p, rs, :] = xv.astype(BF)
+                gs[p, rs, :] = gv.astype(BF)
+
+        @pl.when(t == GAP)
+        def _():
+            wait(nrecv.at[pl.ds(0, NZ), pl.ds(0, NY - 1)], r_n2)
             stage[...] = nrecv[...].reshape(COLS * 16, LANE).astype(F32)
             for r in range(2):
                 for q in range(4):
                     cut = slice(q * LANE, (q + 1) * LANE)
                     rs = slice(r * COLS, (r + 1) * COLS)
-                    xs[0, rs, cut] = stage[pl.ds(r * 4 + q, COLS, stride=16), :].astype(BF)
-                    gs[0, rs, cut] = stage[pl.ds(8 + r * 4 + q, COLS, stride=16), :].astype(BF)
-
-            for i in range(2):
-                xv, gv = hot_rows(0, i)
-                rs = slice(i * 64, (i + 1) * 64)
-                xs[0, rs, :] = (xs[0, rs, :].astype(F32) + xv).astype(BF)
-                gs[0, rs, :] = (gs[0, rs, :].astype(F32) + gv).astype(BF)
-
-        @pl.when(t == 1)
-        def _():
-            ring_wait(1)
-            ring_wait(2)
-
-        @pl.when(t == 2)
-        def _():
-            ring_wait(3)
-
-        @pl.when((t >= 1) & (t < PARTS))
-        def _():
-            for i in range(2):
-                xv, gv = hot_rows(t, i)
-                rs = slice(i * 64, (i + 1) * 64)
-                xs[t, rs, :] = xv.astype(BF)
-                gs[t, rs, :] = gv.astype(BF)
-
-        @pl.when(t < PARTS)
-        def _():
-            partial(t)
+                    xn = stage[pl.ds(r * 4 + q, COLS, stride=16), :]
+                    gn = stage[pl.ds(8 + r * 4 + q, COLS, stride=16), :]
+                    xs[1, rs, cut] = (xs[1, rs, cut].astype(F32) + xn).astype(BF)
+                    gs[1, rs, cut] = (gs[1, rs, cut].astype(F32) + gn).astype(BF)
+
+        @pl.when(due(t, 0))
+        def _():
+            partial(t // GAP)
 
         return carry
 
     lax.fori_loop(0, TICKS, tick, 0)
+
+    xall = xs[...].reshape(PARTS * ROWS, DF)
+    gall = gs[...].reshape(PARTS * ROWS, DF)
+
+    def cols(lo, hi):
+        return ag[:, :, lo:hi].reshape(PARTS * ROWS, hi - lo)
+
+    gga_o[...] = SCALE * t_dot(cols(A_LB, A_LOW), xall).T
+    hb = cols(A_HB, WA)
+    gda_o[...] = SCALE * t_dot(hb, cols(0, HID))[64:128]
+    gdb_o[...] = SCALE * t_dot(hb, gall)[0:64]
 
     for o in range(1, NZ):
         wait(hgot_a.at[o], r_ha.at[o])
-    got = hret[0, :, :, 0:CUT].astype(F32)
+    got = hret[0, 0, :, :, 0:CUT].astype(F32)
     for o in range(1, NZ):
         got = got + hgot_a[o].astype(F32)
     ysend[...] = got.astype(BF)
     for v in range(1, NY):
         to = (y + v) % NY
         push(ysend.at[to], ygot.at[v], s_w, r_w, (z * NY + to, d))
-    for o in range(NZ):
-        wait(hgot_b.at[o, pl.ds(0, NY - 1)], r_hb.at[o])
-        got = hret[o, y, :, CUT:DF].astype(F32)
-        for v in range(1, NY):
-            got = got + hgot_b[o, v].astype(F32)
-        zsend[o] = got.astype(BF)
-        if o > 0:
-            push(zsend.at[o], zgot.at[o], s_v, r_v, (((z + o) % NZ) * NY + y, d))
+    for p in range(PARTS):
+        wait(hgot_b.at[p, pl.ds(0, NY - 1)], r_hb.at[p])
+        for i in range(2):
+            o = offset(p, i)
+            got = hret[p, i, y, :, CUT:DF].astype(F32)
+            for v in range(1, NY):
+                got = got + hgot_b[p, v, i].astype(F32)
+            zsend[o] = got.astype(BF)
+            if o > 0:
+                push(zsend.at[o], zgot.at[o], s_v, r_v, (((z + o) % NZ) * NY + y, d))
     ygot[0] = ysend[y]
     zgot[0] = zsend[0]
 
-    xall = xs[...].reshape(PARTS * ROWS, DF)
-    gall = gs[...].reshape(PARTS * ROWS, DF)
-
-    def cols(lo, hi):
-        return ag[:, :, lo:hi].reshape(PARTS * ROWS, hi - lo)
-
-    gga_o[...] = SCALE * t_dot(cols(A_LB, A_LOW), xall).T
-    hb = cols(A_HB, WA)
     low = cols(A_LOW, A_HB)
     ggb_o[0:64, :] = SCALE * t_dot(low, cols(A_GB, A_GB + HID))[0:64]
     ggb_o[64:128, :] = SCALE * t_dot(low, cols(A_GB + HID, A_LB))[64:128]
-    gda_o[...] = SCALE * t_dot(hb, cols(0, HID))[64:128]
-    gdb_o[...] = SCALE * t_dot(hb, gall)[0:64]
 
     wait(cz.at[pl.ds(0, NZ - 1)], r_cz)
     total = jnp.sum(cz[...].astype(F32).reshape(NZ * 16, LANE), axis=0, keepdims=True)
@@ -463,36 +510,39 @@
     rows_o[0] = rows
     blocks_o[0] = (rows + 127) // 128
 
-    wait(nret.at[pl.ds(0, COLS - 1)], r_b)
+    wait(nret.at[pl.ds(0, NZ - 1)], r_b2)
     stage[...] = nret[...].reshape(COLS * 16, LANE).astype(F32)
+    ordinary = []
+    for q in range(4):
+        mix = jnp.zeros((TOK, LANE), F32)
+        gt = jnp.zeros((TOK, LANE), F32)
+        for r in range(2):
+            rows_out = stage[pl.ds(r * 4 + q, COLS, stride=16), :].astype(BF)
+            rows_dx = stage[pl.ds(8 + r * 4 + q, COLS, stride=16), :].astype(BF)
+            mix = mix + t_dot(route[2 + 2 * r], rows_out) + t_dot(route[3 + 2 * r], rows_out)
+            gt = gt + t_dot(route[r], rows_dx)
+        ordinary.append((mix, gt))
+
     wait(ygot.at[pl.ds(1, NY - 1)], r_w)
     wait(zgot.at[pl.ds(1, NZ - 1)], r_v)
-    back = [ygot[0].astype(F32), zgot[0].astype(F32)]
-    for o in range(1, NY):
-        back[0] = back[0] + ygot[o].astype(F32)
-        back[1] = back[1] + zgot[o].astype(F32)
-
-    def exact(a, b):
-        return lax.dot_general(
-            a, b, (((0,), (0,)), ((), ())),
-            precision=lax.Precision.HIGHEST, preferred_element_type=F32,
-        )
-
-    for q in range(4):
-        cut = slice(q * LANE, (q + 1) * LANE)
-        half = back[q // 2][:, (q % 2) * LANE : (q % 2 + 1) * LANE]
-        mix = exact(hroute[1], half[0:8])
-        gt = exact(hroute[0], half[8:16])
-        for r in range(2):
-            mix = mix + exact(route[2 + r], stage[pl.ds(r * 4 + q, COLS, stride=16), :])
-            gt = gt + t_dot(
-                route[r].astype(BF), stage[pl.ds(8 + r * 4 + q, COLS, stride=16), :].astype(BF)
-            )
-        mixed_o[:, cut] = mix.astype(BF)
-        gtok_o[:, cut] = gt.astype(BF)
-
-    wait(nsend.at[pl.ds(0, COLS - 1)], s_n)
-    wait(nback.at[pl.ds(0, COLS - 1)], s_b)
+    for h, got in enumerate((ygot, zgot)):
+        back = got[0].astype(F32)
+        for o in range(1, NY):
+            back = back + got[o].astype(F32)
+        for q in range(2):
+            cut = slice(q * LANE, (q + 1) * LANE)
+            mix, gt = ordinary[2 * h + q]
+            for r in range(8):
+                mix = mix + hroute[1][:, r : r + 1] * back[r : r + 1, cut]
+                gt = gt + hroute[0][:, r : r + 1] * back[8 + r : 9 + r, cut]
+            at = slice((2 * h + q) * LANE, (2 * h + q + 1) * LANE)
+            mixed_o[:, at] = mix.astype(BF)
+            gtok_o[:, at] = gt.astype(BF)
+
+    wait(nsend.at[pl.ds(0, NZ - 1)], s_n)
+    wait(nmid.at[pl.ds(0, NZ), pl.ds(0, NY - 1)], s_n2)
+    wait(nback.at[pl.ds(0, NZ), pl.ds(0, NY - 1)], s_b)
+    wait(nhalf.at[pl.ds(0, NZ - 1)], s_b2)
     wait(hg.at[z, pl.ds(0, NY - 1)], s_y)
     for h in range(2):
         for s in range(4):
@@ -502,7 +552,7 @@
     wait(cy.at[pl.ds(0, NY - 1)], s_cy)
     wait(cz.at[pl.ds(0, NZ - 1)], s_cz)
     wait(hgot_a.at[pl.ds(1, NZ - 1)], s_ha)
-    wait(hgot_b.at[pl.ds(0, NZ), pl.ds(0, NY - 1)], s_hb)
+    wait(hgot_b.at[pl.ds(0, PARTS), pl.ds(0, NY - 1)], s_hb)
     wait(ysend.at[pl.ds(0, NY - 1)], s_w)
     wait(zsend.at[pl.ds(0, NZ - 1)], s_v)
     for p in range(PARTS):
@@ -558,13 +608,15 @@
             pltpu.VMEM((64, HID), BF),
             pltpu.VMEM((128, DF), BF),
             dma((6,)),
-            pltpu.VMEM((4, COLS, TOK), F32),
-            pltpu.VMEM((2, 8, TOK), F32),
+            pltpu.VMEM((6, COLS, TOK), BF),
+            pltpu.VMEM((2, TOK, 8), F32),
             pltpu.VMEM((COLS * 16, LANE), F32),
-            pltpu.VMEM((COLS, 16, LANE), BF),
-            pltpu.VMEM((COLS, 16, LANE), BF),
-            pltpu.VMEM((COLS, 16, LANE), BF),
-            pltpu.VMEM((COLS, 16, LANE), BF),
+            pltpu.VMEM((NZ, NY, 16, LANE), BF),
+            pltpu.VMEM((NZ, NY, 16, LANE), BF),
+            pltpu.VMEM((NZ, NY, 16, LANE), BF),
+            pltpu.VMEM((NZ, NY, 16, LANE), BF),
+            pltpu.VMEM((NZ, NY, 16, LANE), BF),
+            pltpu.VMEM((NZ, NY, 16, LANE), BF),
             pltpu.VMEM((NZ, NY, 16, DF), BF),
             pltpu.VMEM((PARTS, ROWS, DF), BF),
             pltpu.VMEM((PARTS, ROWS, DF), BF),
@@ -574,19 +626,19 @@
             pltpu.VMEM((PARTS, 2, BLK, HALF), BF),
             pltpu.VMEM((PARTS, 2, BLK, WP), BF),
             pltpu.VMEM((PARTS, ROWS, WA), BF),
-            pltpu.VMEM((NZ, NY, 16, DF), BF),
+            pltpu.VMEM((PARTS, 2, NY, 16, DF), BF),
             pltpu.VMEM((NZ, NY, 16, CUT), BF),
-            pltpu.VMEM((NZ, NY, 16, DF - CUT), BF),
+            pltpu.VMEM((PARTS, NY, 2, 16, DF - CUT), BF),
             pltpu.VMEM((NY, 16, CUT), BF),
             pltpu.VMEM((NY, 16, CUT), BF),
             pltpu.VMEM((NZ, 16, DF - CUT), BF),
             pltpu.VMEM((NZ, 16, DF - CUT), BF),
             pltpu.VMEM((NY, 16, LANE), BF),
             pltpu.VMEM((NZ, 16, LANE), BF),
-            dma, dma, dma, dma, dma, dma,
+            dma, dma, dma, dma, dma, dma, dma, dma, dma, dma,
             dma((4, 2)), dma((4, 2)), dma((3, 2)), dma((3, 2)),
             dma, dma, dma, dma,
-            dma, dma((NZ,)), dma, dma((NZ,)), dma, dma, dma, dma,
+            dma, dma((NZ,)), dma, dma((PARTS,)), dma, dma, dma, dma,
             dma((PARTS,)), dma((PARTS,)),
             dma((PARTS,)), dma((PARTS, 2)), dma((PARTS, 2)),
             dma((PARTS,)), dma((PARTS, 2)), dma((PARTS, 2)),

time: 99.5 us -> 93.9 us (0.944)
  Pallas kernels: 93.8 us -> 88.5 us
    pallas_call x1, Pallas kernels: 91.5 us -> 86.2 us  [per_device(): pl.pallas_call(kernel, out_shape=(jax.ShapeDtypeStruct((TOK, DF), BF), ja...]
where the time goes in v3:
time: 93.9 us; the launch traced here: 92.6 us
  Pallas kernels  88.5 us (94%)
  between operations  4.16 us (4%)
    pallas_call x1, Pallas kernels, per_device(): pl.pallas_call(kernel, out_shape=(jax.ShapeDtypeStruct((TOK, DF), BF), ja...  86.2 us
    pallas_call x1, Pallas kernels, hand_over(): pl.pallas_call(copy_kernel, out_shape=tuple((jax.ShapeDtypeStruct(a.shape...  2.3 us

profile of v3, /device:TPU:6, one launch (start us, length us, event | category | flops | bytes accessed | tf_op | source)
XLA Modules:
  0.0 92.6 jit_solution(393552529311496002)
XLA Ops:
  0.6 86.2 %shard_map.170 = (bf16[16,512]{1,0:T(8,128)(2,1)}, bf16[16,512]{1,0:T(8,128)(2,1)}, f32[512,128]{1,0:T(8,128)}, f32[128,1024]{1,0:T(8,128)}, f32[64,1024]{1,0:T(...) custom-call(bf16[16,512]{1,0:T(8,128)(2,1)} %tok.1, s32[8,16]{1,0:T(8,128)} %bitcast.22, f32[8,16]{1,0:T(8,128)} %bitcast.23, ...), custom_call_target="tpu_custom_call" | custom-call | tf_op jit(solution)/shard_map/pallas_call | solution.py:589
  86.8 2.3 %shard_map.171 = (bf16[16,512]{1,0:T(8,128)(2,1)}, bf16[16,512]{1,0:T(8,128)(2,1)}, f32[512,128]{1,0:T(8,128)}, f32[128,1024]{1,0:T(8,128)}, f32[64,1024]{1,0:T(8,128)}, /*index=5*/f32[64,512]{1,0:T(8,128)}) custom-call(bf16[16,512]{1,0:T(8,128)(2,1)} %get-tuple-element.22.refs_0_, bf16[16,512]{1,0:T(8,128)(2,1)} %get-tuple-element.23.refs_1_, ...), custom_call_target="tpu_custom_call" | custom-call | tf_op jit(solution)/shard_map/pallas_call | solution.py:573

commit v4 on v3

--- a/solution.py
+++ b/solution.py
@@ -127,9 +127,6 @@
     lo, hi = pl.ds(0, CUT), pl.ds(CUT, DF - CUT)
     for o in range(1, NY):
         push(hg.at[z, y], hg.at[z, y], s_y, r_y, (z * NY + (y + o) % NY, d))
-    for o in range(1, NY):
-        push(cy.at[0], cy.at[o], s_cy, r_cy, (z * NY + (y + o) % NY, d))
-
     def keep(at, value):
         head = value.astype(BF)
         route[at] = head
@@ -187,13 +184,8 @@
             (z * NY + (y + o) % NY, d),
         )
     nrecv[:, 0] = nmid[:, 0]
-    wait(cy.at[pl.ds(0, NY - 1)], r_cy)
-    count = cy[0].astype(F32)
     for o in range(1, NY):
-        count = count + cy[o].astype(F32)
-    cz[0] = count.astype(BF)
-    for o in range(1, NZ):
-        push(cz.at[0], cz.at[o], s_cz, r_cz, (((z + o) % NZ) * NY + y, d))
+        push(cy.at[0], cy.at[o], s_cy, r_cy, (z * NY + (y + o) % NY, d))
     for load in loads:
         load.wait()
 
@@ -459,31 +451,21 @@
         def _():
             partial(t // GAP)
 
+        @pl.when(t == 4)
+        def _():
+            wait(cy.at[pl.ds(0, NY - 1)], r_cy)
+            count = cy[0].astype(F32)
+            for o in range(1, NY):
+                count = count + cy[o].astype(F32)
+            cz[0] = count.astype(BF)
+            for o in range(1, NZ):
+                push(cz.at[0], cz.at[o], s_cz, r_cz, (((z + o) % NZ) * NY + y, d))
+
         return carry
 
     lax.fori_loop(0, TICKS, tick, 0)
 
-    xall = xs[...].reshape(PARTS * ROWS, DF)
-    gall = gs[...].reshape(PARTS * ROWS, DF)
-
-    def cols(lo, hi):
-        return ag[:, :, lo:hi].reshape(PARTS * ROWS, hi - lo)
-
-    gga_o[...] = SCALE * t_dot(cols(A_LB, A_LOW), xall).T
-    hb = cols(A_HB, WA)
-    gda_o[...] = SCALE * t_dot(hb, cols(0, HID))[64:128]
-    gdb_o[...] = SCALE * t_dot(hb, gall)[0:64]
-
-    for o in range(1, NZ):
-        wait(hgot_a.at[o], r_ha.at[o])
-    got = hret[0, 0, :, :, 0:CUT].astype(F32)
-    for o in range(1, NZ):
-        got = got + hgot_a[o].astype(F32)
-    ysend[...] = got.astype(BF)
-    for v in range(1, NY):
-        to = (y + v) % NY
-        push(ysend.at[to], ygot.at[v], s_w, r_w, (z * NY + to, d))
-    for p in range(PARTS):
+    def along_y(p):
         wait(hgot_b.at[p, pl.ds(0, NY - 1)], r_hb.at[p])
         for i in range(2):
             o = offset(p, i)
@@ -493,6 +475,31 @@
             zsend[o] = got.astype(BF)
             if o > 0:
                 push(zsend.at[o], zgot.at[o], s_v, r_v, (((z + o) % NZ) * NY + y, d))
+
+    for p in range(PARTS - 1):
+        along_y(p)
+
+    xall = xs[...].reshape(PARTS * ROWS, DF)
+    gall = gs[...].reshape(PARTS * ROWS, DF)
+
+    def cols(lo, hi):
+        return ag[:, :, lo:hi].reshape(PARTS * ROWS, hi - lo)
+
+    gga_o[...] = SCALE * t_dot(cols(A_LB, A_LOW), xall).T
+    hb = cols(A_HB, WA)
+    gda_o[...] = SCALE * t_dot(hb, cols(0, HID))[64:128]
+    gdb_o[...] = SCALE * t_dot(hb, gall)[0:64]
+
+    order = [offset(p, i) for p in range(PARTS) for i in range(2)]
+    got = hret[0, 0, :, :, 0:CUT].astype(F32)
+    for o in order[1:]:
+        wait(hgot_a.at[o], r_ha.at[o])
+        got = got + hgot_a[o].astype(F32)
+    ysend[...] = got.astype(BF)
+    for v in range(1, NY):
+        to = (y + v) % NY
+        push(ysend.at[to], ygot.at[v], s_w, r_w, (z * NY + to, d))
+    along_y(PARTS - 1)
     ygot[0] = ysend[y]
     zgot[0] = zsend[0]
 

time: 93.9 us -> 93.4 us (level)
  no operation moved by 1% of the time
where the time goes in v4:
time: 93.4 us; the launch traced here: 92 us
  Pallas kernels  87.8 us (94%)
  between operations  4.16 us (4%)
    pallas_call x1, Pallas kernels, per_device(): pl.pallas_call(kernel, out_shape=(jax.ShapeDtypeStruct((TOK, DF), BF), ja...  85.5 us
    pallas_call x1, Pallas kernels, hand_over(): pl.pallas_call(copy_kernel, out_shape=tuple((jax.ShapeDtypeStruct(a.shape...  2.3 us

profile of v4, /device:TPU:6, one launch (start us, length us, event | category | flops | bytes accessed | tf_op | source)
XLA Modules:
  0.0 92.0 jit_solution(17570766914922248720)
XLA Ops:
  0.6 85.5 %shard_map.170 = (bf16[16,512]{1,0:T(8,128)(2,1)}, bf16[16,512]{1,0:T(8,128)(2,1)}, f32[512,128]{1,0:T(8,128)}, f32[128,1024]{1,0:T(8,128)}, f32[64,1024]{1,0:T(...) custom-call(bf16[16,512]{1,0:T(8,128)(2,1)} %tok.1, s32[8,16]{1,0:T(8,128)} %bitcast.22, f32[8,16]{1,0:T(8,128)} %bitcast.23, ...), custom_call_target="tpu_custom_call" | custom-call | tf_op jit(solution)/shard_map/pallas_call | solution.py:596
  86.2 2.3 %shard_map.171 = (bf16[16,512]{1,0:T(8,128)(2,1)}, bf16[16,512]{1,0:T(8,128)(2,1)}, f32[512,128]{1,0:T(8,128)}, f32[128,1024]{1,0:T(8,128)}, f32[64,1024]{1,0:T(8,128)}, /*index=5*/f32[64,512]{1,0:T(8,128)}) custom-call(bf16[16,512]{1,0:T(8,128)(2,1)} %get-tuple-element.22.refs_0_, bf16[16,512]{1,0:T(8,128)(2,1)} %get-tuple-element.23.refs_1_, ...), custom_call_target="tpu_custom_call" | custom-call | tf_op jit(solution)/shard_map/pallas_call | solution.py:580
